TPU v7x, 512 devices: a whole 4x8x8 slice. The times are simulated.
512 devices in a mesh: tm: 128 (over y, z, x_lo), batch: 4 (over x_hi, core).
Axes of the slice: x: 4 (x_hi: 2, x_lo: 2; x = x_hi * 2 + x_lo), y: 8, z: 8, core: 2. Of those that a mesh axis runs over, the one named last changes fastest.
Arguments:
- signal: bfloat16 [16, 16384, 64], P('batch', 'tm'), may hold values from -6 to 6
- skip_grad: bfloat16 [16, 16384, 128], P('batch', 'tm'), may hold values from -24 to 24
- stream_grad: bfloat16 [16, 16384, 64], P('batch', 'tm'), may hold values from -24 to 24
- w_past: bfloat16 [5, 64, 512], replicated, may hold values from -0.5 to 0.5
- w_now: bfloat16 [5, 64, 512], replicated, may hold values from -0.5 to 0.5
- w_res: bfloat16 [5, 256, 64], replicated, may hold values from -0.375 to 0.375
- w_skip: bfloat16 [5, 256, 128], replicated, may hold values from -0.375 to 0.375
Outputs:
- skip_out: bfloat16 [16, 16384, 128], P('batch', 'tm')
- stream_out: bfloat16 [16, 16384, 64], P('batch', 'tm')
- signal_cot: bfloat16 [16, 16384, 64], P('batch', 'tm')
- g_past: bfloat16 [5, 64, 512], replicated
- g_now: bfloat16 [5, 64, 512], replicated
- g_res: bfloat16 [5, 256, 64], replicated
- g_skip: bfloat16 [5, 256, 128], replicated
All inputs are finite; a program needn't handle non-finite values.
Results may differ from a plain program's by a relative error of at most 0.015.
Values may be sent and summed in bfloat16 or wider, within the bound.
A program may use at most 64 MiB of HBM per device.

v0:
```python
import math

import jax
import jax.numpy as jnp
from jax import lax
from jax.sharding import PartitionSpec as P


def from_behind(block, axis, distance):
    devices = range(lax.axis_size(axis))
    route = [(i - distance, i) for i in devices if i - distance in devices]
    return lax.ppermute(block, axis, route)


def product(left, right):
    return jnp.einsum("str,rc->stc", left, right, preferred_element_type=jnp.float32)


def product_transposed(left, right):
    return jnp.einsum("stc,rc->str", left, right, preferred_element_type=jnp.float32)


def column_sum(left, right):
    return jnp.einsum("str,stc->rc", left, right, preferred_element_type=jnp.float32)


def forward_layer(stream, delayed, layer, w_past, w_now, w_res, w_skip, records, skip_acc):
    gate_width = w_res.shape[1]
    preact = product(delayed, w_past[layer]) + product(stream, w_now[layer])
    gated = (
        jnp.tanh(preact[:, :, :gate_width]) * jax.nn.sigmoid(preact[:, :, gate_width:])
    ).astype(jnp.bfloat16)
    records.append((delayed, stream, preact, gated))
    skip_acc = skip_acc + product(gated, w_skip[layer])
    stream = (stream.astype(jnp.float32) + product(gated, w_res[layer])).astype(jnp.bfloat16)
    return (stream, skip_acc)


def on_device(signal, skip_grad, stream_grad, w_past, w_now, w_res, w_skip):
    stream = signal
    seq_count = stream.shape[0]
    rows = stream.shape[1]
    base_step = rows // 16
    layers = w_past.shape[0]
    gate_width = w_res.shape[1]
    near_layers = 4
    records = []
    skip_acc = jnp.zeros((seq_count, rows, w_skip.shape[2]), jnp.float32)
    for layer in range(near_layers):
        dilation = base_step * 2**layer
        edge_rows = from_behind(stream[:, rows - dilation :], "tm", 1)
        delayed = jnp.concatenate([edge_rows, stream[:, : rows - dilation]], 1)
        stream, skip_acc = forward_layer(
            stream, delayed, layer, w_past, w_now, w_res, w_skip, records, skip_acc
        )
    layer = 4
    hops = base_step * 2**layer // rows
    delayed = from_behind(stream, "tm", hops)
    stream, skip_acc = forward_layer(
        stream, delayed, layer, w_past, w_now, w_res, w_skip, records, skip_acc
    )
    skip_out = skip_acc.astype(jnp.bfloat16)
    flow = stream_grad.astype(jnp.float32)
    grads = [None] * layers
    for layer in reversed(range(layers)):
        dilation = base_step * 2**layer
        delayed, current, preact, gated = records[layer]
        filt = jnp.tanh(preact[:, :, :gate_width])
        sigm = jax.nn.sigmoid(preact[:, :, gate_width:])
        flow_half = flow.astype(jnp.bfloat16)
        gated_cot = product_transposed(skip_grad, w_skip[layer]) + product_transposed(
            flow_half, w_res[layer]
        )
        pre_cot = jnp.concatenate(
            [gated_cot * sigm * (1.0 - filt * filt), gated_cot * filt * sigm * (1.0 - sigm)], 2
        ).astype(jnp.bfloat16)
        local_grads = (
            column_sum(delayed, pre_cot),
            column_sum(current, pre_cot),
            column_sum(gated, flow_half),
            column_sum(gated, skip_grad),
        )
        grads[layer] = local_grads
        past_cot = product_transposed(pre_cot, w_past[layer]).astype(jnp.bfloat16)
        if dilation < rows:
            head_rows = from_behind(past_cot[:, :dilation], "tm", -1)
            moved = jnp.concatenate([past_cot[:, dilation:], head_rows], 1)
        else:
            moved = from_behind(past_cot, "tm", -(dilation // rows))
        flow = flow + product_transposed(pre_cot, w_now[layer]) + moved.astype(jnp.float32)
    signal_cot = flow.astype(jnp.bfloat16)
    stacked = tuple(
        (jnp.stack([grads[layer][which] for layer in range(layers)]) for which in range(4))
    )
    scale = 1.0 / math.sqrt(seq_count * lax.axis_size("batch") * rows * lax.axis_size("tm"))
    totals = lax.psum(stacked, ("tm", "batch"))
    finals = tuple(((total * scale).astype(jnp.bfloat16) for total in totals))
    return (skip_out, stream, signal_cot, finals[0], finals[1], finals[2], finals[3])


def solution(mesh):
    placed = (
        P("batch", "tm", None),
        P("batch", "tm", None),
        P("batch", "tm", None),
        P(),
        P(),
        P(),
        P(),
    )
    return jax.shard_map(
        on_device,
        mesh=mesh,
        in_specs=placed,
        out_specs=(
            P("batch", "tm", None),
            P("batch", "tm", None),
            P("batch", "tm", None),
            P(),
            P(),
            P(),
            P(),
        ),
        check_vma=False,
    )
```

profile of v0, /device:TPU:1, one launch (start us, length us, event | category | flops | bytes accessed | tf_op | source)
XLA Modules:
  0.0 406.1 jit_solution(14410823166842004948)
XLA Ops:
  7.2 1.0 slice.168
  8.2 4.1 %collective-permute-start = (bf16[4,8,64]{1,2,0:T(8,128)(2,1)S(1)}, bf16[4,8,64]{1,2,0:T(8,128)(2,1)S(1)}, u32[]{:S(2)}, u32[]{:S(2)}) collective-permute-start(bf16[4,8,64]{1,2,0:T(8,128)(2,1)S(1)} %slice.168), channel_id=1, source_target_pairs={{0,4},{4,8},{8,12},{12,16},{16,20},{20,24},{24,28},{28,32},{32,36}... | collective-permute-start | bytes 12296 | tf_op jit(solution)/shard_map/ppermute | solution.py:12
  12.3 1.1 fusion.46
  14.1 0.6 copy-done.2
  15.4 0.7 copy-done.9
  16.1 0.4 convolution_add_fusion.4
  17.0 0.7 copy-done.11
  17.9 0.3 fusion.74
  18.3 4.0 collective-permute-start.1
  22.6 1.0 collective-permute-done.1
  23.6 0.4 convolution_add_fusion.3
  24.4 0.3 fusion.66
  25.1 3.7 collective-permute-start.2
  29.0 1.0 collective-permute-done.2
  30.1 0.4 convolution_add_fusion.2
  31.0 4.0 collective-permute-start.3
  35.4 1.0 collective-permute-done.3
  36.4 0.4 convolution_add_fusion.1
  37.2 4.6 %collective-permute-start.4 = (bf16[4,128,64]{1,2,0:T(8,128)(2,1)S(1)}, bf16[4,128,64]{1,2,0:T(8,128)(2,1)S(1)}, u32[]{:S(2)}, u32[]{:S(2)}) collective-permute-start(bf16[4,128,64]{1,2,0:T(8,128)(2,1)S(1)} %fusion.23), channel_id=1, source_target_pairs={{0,4},{4,8},{8,12},{12,16},{16,20},{20,24},{24,28},{28,32},{32,36}... | collective-permute-start | bytes 196616 | tf_op jit(solution)/shard_map/ppermute | solution.py:12
  41.8 0.3 fusion.50
  42.1 1.0 collective-permute-done.4
  43.1 0.3 convolution_add_fusion
  43.4 0.5 multiply_convert_fusion.12
  44.2 1.3 collective-permute-start.5
  45.7 4.7 %collective-permute-done.5 = bf16[4,128,64]{1,2,0:T(8,128)(2,1)S(1)} collective-permute-done((bf16[4,128,64]{1,2,0:T(8,128)(2,1)S(1)}, bf16[4,128,64]{1,2,0:T(8,128)(2,1)S(1)}, u32[]{:S(2)}, u32[]{:S(2)}) %collective-permute-start.5) | collective-permute-done | bytes 65568 | tf_op jit(solution)/shard_map/ppermute | solution.py:12
  50.7 0.4 multiply_convert_fusion.10
  51.5 1.3 collective-permute-start.6
  53.1 4.7 %collective-permute-done.6 = bf16[4,64,64]{1,2,0:T(8,128)(2,1)S(1)} collective-permute-done((bf16[4,64,64]{1,2,0:T(8,128)(2,1)S(1)}, bf16[4,64,64]{1,2,0:T(8,128)(2,1)S(1)}, u32[]{:S(2)}, u32[]{:S(2)}) %collective-permute-start.6) | collective-permute-done | bytes 32800 | tf_op jit(solution)/shard_map/ppermute | solution.py:12
  58.0 0.4 multiply_convert_fusion.8
  58.8 1.3 collective-permute-start.7
  60.4 4.6 %collective-permute-done.7 = bf16[4,32,64]{1,2,0:T(8,128)(2,1)S(1)} collective-permute-done((bf16[4,32,64]{1,2,0:T(8,128)(2,1)S(1)}, bf16[4,32,64]{1,2,0:T(8,128)(2,1)S(1)}, u32[]{:S(2)}, u32[]{:S(2)}) %collective-permute-start.7) | collective-permute-done | bytes 16416 | tf_op jit(solution)/shard_map/ppermute | solution.py:12
  65.3 0.4 multiply_convert_fusion.6
  66.0 1.3 collective-permute-start.8
  67.7 5.2 %collective-permute-done.8 = bf16[4,16,64]{1,2,0:T(8,128)(2,1)S(1)} collective-permute-done((bf16[4,16,64]{1,2,0:T(8,128)(2,1)S(1)}, bf16[4,16,64]{1,2,0:T(8,128)(2,1)S(1)}, u32[]{:S(2)}, u32[]{:S(2)}) %collective-permute-start.8) | collective-permute-done | bytes 8224 | tf_op jit(solution)/shard_map/ppermute | solution.py:12
  73.4 0.5 copy-done.12
  73.9 0.4 multiply_convert_fusion.4
  76.0 0.3 copy-done.7
  76.7 0.5 copy-done.8
  78.2 0.8 copy-done.6
  79.3 0.9 fusion
  80.6 1.3 collective-permute-start.9
  81.9 0.8 fusion.24
  82.8 3.2 collective-permute-done.9
  86.0 1.8 fusion.25
  87.7 306.8 %all-reduce.3.cloned.1.call-done = (f32[5,64,512]{2,1,0:T(8,128)}, f32[5,64,512]{2,1,0:T(8,128)}, f32[5,256,64]{1,2,0:T(8,128)}, f32[5,256,128]{2,1,0:T(8,128)}) async-done(((f32[5,64,512]{2,1,0:T(8,128)}, f32[5,64,512]{2,1,0:T(8,128)}, f32[5,256,64]{1,2,0:T(8,128)}, f32[5,256,128]{2,1,0:T(8,128)}), (f32[5,64,512]{2,1,0:T(8,128)}, f32[5,64,512]{2,1,0:T(8,128)}, f32[5,256,64]{1,2,0:T(8,128)}, ...) | async-done | bytes 2293776 | tf_op jit(solution)/shard_map/psum | solution.py:96
  394.6 1.8 multiply_convert_fusion.18
  396.4 1.9 multiply_convert_fusion
  398.2 1.0 multiply_convert_fusion.1
  (88 shorter events, 12.1 us)
Async XLA Ops:
  7.2 5.1 %copy-start = (bf16[4,128,128]{2,1,0:T(8,128)(2,1)S(1)}, bf16[4,128,128]{2,1,0:T(8,128)(2,1)}, u32[]{:S(2)}) copy-start(bf16[4,128,128]{2,1,0:T(8,128)(2,1)} %param.8) | copy-start | bytes 393220
  7.2 387.4 %all-reduce.3.cloned.1.call-start = ((), (), s32[]{:S(2)}) async-start(), calls=%async_computation | async-start | bytes 4587520 | tf_op jit(solution)/shard_map/psum | solution.py:96
  8.2 5.2 %copy-start.1 = (bf16[5,256,128]{2,1,0:T(8,128)(2,1)S(1)}, bf16[5,256,128]{2,1,0:T(8,128)(2,1)}, u32[]{:S(2)}) copy-start(bf16[5,256,128]{2,1,0:T(8,128)(2,1)} %param.13) | copy-start | bytes 983044
  8.2 7.2 %collective-permute-start = (bf16[4,8,64]{1,2,0:T(8,128)(2,1)S(1)}, bf16[4,8,64]{1,2,0:T(8,128)(2,1)S(1)}, u32[]{:S(2)}, u32[]{:S(2)}) collective-permute-start(bf16[4,8,64]{1,2,0:T(8,128)(2,1)S(1)} %slice.168), channel_id=1, source_target_pairs={{0,4},{4,8},{8,12},{12,16},{16,20},{20,24},{24,28},{28,32},{32,36}... | collective-permute-start | bytes 12296 | tf_op jit(solution)/shard_map/ppermute | solution.py:12
  13.8 0.8 copy-start.2
  13.8 1.0 copy-start.10
  15.2 1.0 copy-start.9
  16.8 0.9 copy-start.11
  18.3 5.3 %collective-permute-start.1 = (bf16[4,16,64]{1,2,0:T(8,128)(2,1)S(1)}, bf16[4,16,64]{1,2,0:T(8,128)(2,1)S(1)}, u32[]{:S(2)}, u32[]{:S(2)}) collective-permute-start(bf16[4,16,64]{1,2,0:T(8,128)(2,1)S(1)} %slice.216), channel_id=1, source_target_pairs={{0,4},{4,8},{8,12},{12,16},{16,20},{20,24},{24,28},{28,32},{32,36}... | collective-permute-start | bytes 24584 | tf_op jit(solution)/shard_map/ppermute | solution.py:12
  25.1 5.0 %collective-permute-start.2 = (bf16[4,32,64]{1,2,0:T(8,128)(2,1)S(1)}, bf16[4,32,64]{1,2,0:T(8,128)(2,1)S(1)}, u32[]{:S(2)}, u32[]{:S(2)}) collective-permute-start(bf16[4,32,64]{1,2,0:T(8,128)(2,1)S(1)} %slice.220), channel_id=1, source_target_pairs={{0,4},{4,8},{8,12},{12,16},{16,20},{20,24},{24,28},{28,32},{32,36}... | collective-permute-start | bytes 49160 | tf_op jit(solution)/shard_map/ppermute | solution.py:12
  31.0 5.4 %collective-permute-start.3 = (bf16[4,64,64]{1,2,0:T(8,128)(2,1)S(1)}, bf16[4,64,64]{1,2,0:T(8,128)(2,1)S(1)}, u32[]{:S(2)}, u32[]{:S(2)}) collective-permute-start(bf16[4,64,64]{1,2,0:T(8,128)(2,1)S(1)} %get-tuple-element.24), channel_id=1, source_target_pairs={{0,4},{4,8},{8,12},{12,16},{16,20},{20,24},{24,28},{28,32},{32,36}... | collective-permute-start | bytes 98312 | tf_op jit(solution)/shard_map/ppermute | solution.py:12
  37.2 5.9 %collective-permute-start.4 = (bf16[4,128,64]{1,2,0:T(8,128)(2,1)S(1)}, bf16[4,128,64]{1,2,0:T(8,128)(2,1)S(1)}, u32[]{:S(2)}, u32[]{:S(2)}) collective-permute-start(bf16[4,128,64]{1,2,0:T(8,128)(2,1)S(1)} %fusion.23), channel_id=1, source_target_pairs={{0,4},{4,8},{8,12},{12,16},{16,20},{20,24},{24,28},{28,32},{32,36}... | collective-permute-start | bytes 196616 | tf_op jit(solution)/shard_map/ppermute | solution.py:12
  42.1 1.3 copy-start.14
  44.2 6.2 %collective-permute-start.5 = (bf16[4,128,64]{1,2,0:T(8,128)(2,1)S(1)}, bf16[4,128,64]{1,2,0:T(8,128)(2,1)S(1)}, u32[]{:S(2)}, u32[]{:S(2)}) collective-permute-start(bf16[4,128,64]{1,2,0:T(8,128)(2,1)S(1)} %convolution_convert_fusion.4), channel_id=1, source_target_pairs={{4,0},{8,4},{12,8},{16,12},{20,16},{24,20},{28,24},{32,28},{36,32}... | collective-permute-start | bytes 196616 | tf_op jit(solution)/shard_map/ppermute | solution.py:12
  51.5 6.2 %collective-permute-start.6 = (bf16[4,64,64]{1,2,0:T(8,128)(2,1)S(1)}, bf16[4,64,64]{1,2,0:T(8,128)(2,1)S(1)}, u32[]{:S(2)}, u32[]{:S(2)}) collective-permute-start(bf16[4,64,64]{1,2,0:T(8,128)(2,1)S(1)} %get-tuple-element.23), channel_id=1, source_target_pairs={{4,0},{8,4},{12,8},{16,12},{20,16},{24,20},{28,24},{32,28},{36,32}... | collective-permute-start | bytes 98312 | tf_op jit(solution)/shard_map/ppermute | solution.py:12
  58.8 6.3 %collective-permute-start.7 = (bf16[4,32,64]{1,2,0:T(8,128)(2,1)S(1)}, bf16[4,32,64]{1,2,0:T(8,128)(2,1)S(1)}, u32[]{:S(2)}, u32[]{:S(2)}) collective-permute-start(bf16[4,32,64]{1,2,0:T(8,128)(2,1)S(1)} %bitcast.291), channel_id=1, source_target_pairs={{4,0},{8,4},{12,8},{16,12},{20,16},{24,20},{28,24},{32,28},{36,32}... | collective-permute-start | bytes 49160 | tf_op jit(solution)/shard_map/ppermute | solution.py:12
  66.0 6.9 %collective-permute-start.8 = (bf16[4,16,64]{1,2,0:T(8,128)(2,1)S(1)}, bf16[4,16,64]{1,2,0:T(8,128)(2,1)S(1)}, u32[]{:S(2)}, u32[]{:S(2)}) collective-permute-start(bf16[4,16,64]{1,2,0:T(8,128)(2,1)S(1)} %bitcast.289), channel_id=1, source_target_pairs={{4,0},{8,4},{12,8},{16,12},{20,16},{24,20},{28,24},{32,28},{36,32}... | collective-permute-start | bytes 24584 | tf_op jit(solution)/shard_map/ppermute | solution.py:12
  67.6 5.8 %copy-start.3 = (f32[5,256,128]{2,1,0:T(8,128)}, f32[5,256,128]{2,1,0:T(8,128)S(1)}, u32[]{:S(2)}) copy-start(f32[5,256,128]{2,1,0:T(8,128)S(1)} %fusion.2) | copy-start | bytes 1966084
  73.3 0.7 copy-start.12
  74.3 2.1 copy-start.15
  74.4 2.1 copy-start.17
  75.4 0.8 copy-start.7
  76.5 0.7 copy-start.8
  78.2 0.8 copy-start.6
  79.3 1.0 copy-start.16
  79.3 1.0 copy-start.18
  80.6 5.4 %collective-permute-start.9 = (bf16[4,8,64]{1,2,0:T(8,128)(2,1)S(1)}, bf16[4,8,64]{1,2,0:T(8,128)(2,1)S(1)}, u32[]{:S(2)}, u32[]{:S(2)}) collective-permute-start(bf16[4,8,64]{1,2,0:T(8,128)(2,1)S(1)} %bitcast.290), channel_id=1, source_target_pairs={{4,0},{8,4},{12,8},{16,12},{20,16},{24,20},{28,24},{32,28},{36,32}... | collective-permute-start | bytes 12296 | tf_op jit(solution)/shard_map/ppermute | solution.py:12
  82.7 3.3 copy-start.13
  394.6 3.6 copy-start.4
  394.6 3.6 copy-start.5
Sparse Core Ops, SparseCore 0:
  79.1 315.3 all-reduce.2
where the time goes:
time: 408 us; the launch traced here: 406 us
  waiting for transfers between devices  333 us (82%)
  starting transfers between devices  26.9 us (7%)
  matrix products  19.7 us (5%)
  between operations  14.6 us (4%)
  local copies, waits for them, and re-layouts  6.03 us (1%)
  other arithmetic  5.5 us (1%)
    psum x1, waiting for transfers between devices, on_device(): totals = lax.psum(stacked, ('tm', 'batch'))  307 us
    ppermute x10, starting transfers between devices, from_behind(): return lax.ppermute(block, axis, route)  26.8 us
    ppermute x10, waiting for transfers between devices, from_behind(): return lax.ppermute(block, axis, route)  26.5 us
    dot_general x20, matrix products, product_transposed(): jnp.einsum('stc,rc->str', left, right, preferred_element_type=jnp.float32)  8.41 us
  transfers between devices with their start and end apart: 11, of which 10 were waited for; matrix products, arithmetic and copies ran while one was open for 2% of the time, Pallas kernels for 0%

commit v1 on v0

v1 whole, which is shorter than its diff:
```python
import functools
import math

import jax
import jax.numpy as jnp
from jax import lax
from jax.experimental import pallas as pl
from jax.experimental.pallas import tpu as pltpu
from jax.sharding import PartitionSpec as P

MESH = pl.DeviceIdType.MESH
F32 = jnp.float32
BF16 = jnp.bfloat16

RES = 64
GATE = 256
SKIP = 128
LAYERS = 5
SEQ = 4
ROWS = 128
N = SEQ * ROWS
DIL = (8, 16, 32, 64, 128)
LOW = (16, 32, 64, 128, 128)
CHUNK = 32
GROUP = 8
TILES = 8
WIRE = 7


def nn(left, right):
    return jnp.dot(left, right, preferred_element_type=F32)


def nt(left, right):
    return lax.dot_general(left, right, (((1,), (1,)), ((), ())), preferred_element_type=F32)


def tn(left, right):
    return lax.dot_general(left, right, (((0,), (0,)), ((), ())), preferred_element_type=F32)


def kernel(
    ny, nz, scale,
    signal, skip_grad, stream_grad, w_past, w_now, w_res, w_skip,
    skip_out, stream_out, signal_cot, g_past, g_now, g_res, g_skip,
    wx, wb, wf, wg, h2, xs, pre, gat_ext, gated, dfilt, dgate, skip_acc, flow, gcot, ycat, pcot,
    sig_in, h4_out, h4_in, past_out, past_in,
    grad, rs_in, part, part_in, line_in, final,
    halo_send, halo_recv, red_send, red_recv,
):
    tm = lax.axis_index("tm")
    batch = lax.axis_index("batch")
    blocks = ny * nz * 2
    x_lo = tm % 2
    zi = (tm // 2) % nz
    yi = tm // (2 * nz)
    ei = batch * 2 + x_lo
    tz = TILES // nz

    after = {"tm": (tm + 1) % blocks, "batch": batch}
    before = {"tm": (tm + blocks - 1) % blocks, "batch": batch}

    def group_peer(r):
        e = (ei + r) % GROUP
        return e, {"tm": tm - x_lo + e % 2, "batch": e // 2}

    def z_peer(r):
        z = (zi + r) % nz
        return z, {"tm": (yi * nz + z) * 2 + x_lo, "batch": batch}

    def y_peer(r):
        y = (yi + r) % ny
        return y, {"tm": (y * nz + zi) * 2 + x_lo, "batch": batch}

    partners = [after, before]
    partners += [group_peer(r)[1] for r in range(1, GROUP)]
    partners += [z_peer(r)[1] for r in range(1, nz)]
    partners += [y_peer(r)[1] for r in range(1, ny)]
    barrier = pltpu.get_barrier_semaphore()
    for partner in partners:
        pl.semaphore_signal(barrier, inc=1, device_id=partner, device_id_type=MESH)

    twice = (
        lax.broadcasted_iota(jnp.int32, (RES, 128), 1) % RES
        == lax.broadcasted_iota(jnp.int32, (RES, 128), 0)
    ).astype(F32).astype(BF16)
    low_half = lax.broadcasted_iota(jnp.int32, (1, 128), 1) < RES
    for j in range(LAYERS):
        wx[j, 0:64, :] = w_past[j]
        wx[j, 64:128, :] = w_now[j]
        wb[j, 0:64, :] = w_past[j]
        wb[j, 64:128, :] = w_past[j]
        wb[j, 128:192, :] = w_now[j]
        wb[j, 192:256, :] = w_now[j]
        wf[j, :, 0:128] = w_skip[j]
        wg[j, :, 0:128] = w_skip[j]
        both = nn(w_res[j], twice)
        wf[j, :, 128:256] = both.astype(BF16)
        wg[j, :, 128:256] = jnp.where(low_half, both, 0.0).astype(BF16)
    h2[0, :, 128:256, :] = nn(signal[...].reshape(N, RES), twice).reshape(SEQ, ROWS, 128)
    ycat[:, 0:128] = skip_grad[...].reshape(N, SKIP)
    flow[...] = nn(stream_grad[...].reshape(N, RES), twice)

    pl.semaphore_wait(barrier, len(partners))

    def halo_copy(which, src, dst, target):
        return pltpu.make_async_remote_copy(
            src_ref=src, dst_ref=dst, send_sem=halo_send.at[which], recv_sem=halo_recv.at[which],
            device_id=target, device_id_type=MESH,
        )

    first = halo_copy(5, signal, sig_in, after)
    first.start()
    has_before = jnp.where(tm > 0, 1.0, 0.0).astype(F32)
    has_after = jnp.where(tm < blocks - 1, 1.0, 0.0).astype(F32)
    skip_acc[...] = jnp.zeros_like(skip_acc)
    first.wait()
    h2[0, :, 0:128, :] = has_before * nn(sig_in[...].reshape(N, RES), twice).reshape(SEQ, ROWS, 128)

    def forward_rows(j, lo, hi):
        own = lo == 128
        span = hi - lo
        count = SEQ * span
        d = DIL[j]
        x = jnp.where(low_half, h2[j, :, lo - d : hi - d, :], h2[j, :, lo:hi, :])
        x = x.reshape(count, 128).astype(BF16)
        if own:
            xs[j] = x
        pre[0:count, :] = nn(x, wx[j])

        def step(i, carry):
            rows = pl.ds(pl.multiple_of(i * CHUNK, CHUNK), CHUNK)
            t = jnp.tanh(pre[rows, 0:GATE])
            s = 0.5 * jnp.tanh(0.5 * pre[rows, GATE : 2 * GATE]) + 0.5
            ts = t * s
            if own:
                gated[j, rows, :] = ts.astype(BF16)
                dfilt[j, rows, :] = s * (1.0 - t * t)
                dgate[j, rows, :] = ts * (1.0 - s)
            else:
                gat_ext[rows, :] = ts.astype(BF16)
            return carry

        lax.fori_loop(0, count // CHUNK, step, 0)
        g = gated[j] if own else gat_ext[0:count, :]
        y = nn(g, wf[j])
        if own:
            skip_acc[...] += y[:, 0:128]
        new = h2[j, :, lo:hi, :].reshape(count, 128) + y[:, 128:256]
        new = new.astype(BF16)
        if j + 1 < LAYERS:
            h2[j + 1, :, lo:hi, :] = new.astype(F32).reshape(SEQ, span, 128)
        return new

    for j in range(4):
        if LOW[j] < 128:
            forward_rows(j, LOW[j], 128)
        new = forward_rows(j, 128, 256)
    h4_out[...] = new.reshape(SEQ, ROWS, 128)
    second = halo_copy(6, h4_out, h4_in, after)
    second.start()
    second.wait()
    h2[4, :, 0:128, :] = has_before * h4_in[...].astype(F32)
    new = forward_rows(4, 128, 256)
    stream_out[...] = new[:, 0:RES].reshape(SEQ, ROWS, RES)
    skip_out[...] = skip_acc[...].astype(BF16).reshape(SEQ, ROWS, SKIP)

    def red_copy(stage, j, src, dst, target):
        pltpu.make_async_remote_copy(
            src_ref=src, dst_ref=dst, send_sem=red_send.at[stage, j], recv_sem=red_recv.at[stage, j],
            device_id=target, device_id_type=MESH,
        ).start()

    def red_wait(sem, ref):
        pltpu.make_async_copy(ref, ref, sem).wait()

    def exchange_a(j):
        for r in range(1, GROUP):
            e, peer = group_peer(r)
            red_copy(0, j, grad.at[j, e], rs_in.at[j, r - 1], peer)

    def exchange_b(j):
        red_wait(red_recv.at[0, j], rs_in.at[j])
        total = grad[j, ei].astype(F32)
        for r in range(GROUP - 1):
            total += rs_in[j, r].astype(F32)
        for k in range(WIRE):
            part[j, k // tz, k % tz] = total[:, 128 * k : 128 * k + 128].astype(BF16)
        for k in range(WIRE, TILES):
            part[j, k // tz, k % tz] = jnp.zeros((16, 128), BF16)
        for r in range(1, nz):
            z, peer = z_peer(r)
            red_copy(1, j, part.at[j, z], part_in.at[j, r - 1], peer)

    def exchange_c(j):
        if nz > 1:
            red_wait(red_recv.at[1, j], part_in.at[j])
        total = part[j, zi].astype(F32)
        for r in range(nz - 1):
            total += part_in[j, r].astype(F32)
        line_in[j, yi] = total.astype(BF16)
        for r in range(1, ny):
            _, peer = y_peer(r)
            red_copy(2, j, line_in.at[j, yi], line_in.at[j, yi], peer)

    def exchange_d(j):
        if ny > 1:
            red_wait(red_recv.at[2, j], line_in.at[j, pl.ds(0, ny - 1)])
        total = line_in[j, 0].astype(F32)
        for r in range(1, ny):
            total += line_in[j, r].astype(F32)
        final[j, ei, zi] = (total * scale).astype(BF16)
        for r in range(1, nz):
            _, peer = z_peer(r)
            red_copy(3, j, final.at[j, ei, zi], final.at[j, ei, zi], peer)

    def exchange_e(j):
        if nz > 1:
            red_wait(red_recv.at[3, j], final.at[j, 0, pl.ds(0, nz - 1)])
        for r in range(1, GROUP):
            _, peer = group_peer(r)
            red_copy(4, j, final.at[j, ei], final.at[j, ei], peer)

    def finish(j):
        red_wait(red_recv.at[4, j], final.at[j, pl.ds(0, GROUP - 1)])
        tile = [final[j, :, k // tz, k % tz].reshape(128, 128) for k in range(WIRE)]
        for k in range(4):
            g_past[j, :, 128 * k : 128 * k + 128] = tile[k][0:64]
            g_now[j, :, 128 * k : 128 * k + 128] = tile[k][64:128]
        g_res[j, 0:128, :] = tile[4][:, 0:RES]
        g_res[j, 128:256, :] = pltpu.roll(tile[4].astype(F32), RES, 1)[:, 0:RES].astype(BF16)
        g_skip[j, 0:128, :] = tile[5]
        g_skip[j, 128:256, :] = tile[6]

    stages = (exchange_a, exchange_b, exchange_c, exchange_d, exchange_e, finish)

    for j in reversed(range(LAYERS)):
        d = DIL[j]
        head = max(d, 16)
        ycat[:, 128:256] = flow[...].astype(BF16)
        gcot[...] = nt(ycat[...], wg[j])

        def step(i, carry, j=j):
            rows = pl.ds(pl.multiple_of(i * CHUNK, CHUNK), CHUNK)
            gc = gcot[rows, :]
            pcot[rows, 0:GATE] = (gc * dfilt[j, rows, :]).astype(BF16)
            pcot[rows, GATE : 2 * GATE] = (gc * dgate[j, rows, :]).astype(BF16)
            return carry

        lax.fori_loop(0, N // CHUNK, step, 0)
        back = nt(pcot[...], wb[j])
        past = back[:, 0:128].astype(BF16).reshape(SEQ, ROWS, 128)
        past_out[j, :, 0:head, :] = past[:, 0:head, :]
        third = halo_copy(
            j, past_out.at[j, :, pl.ds(0, head), :], past_in.at[j, :, pl.ds(0, head), :], before
        )
        third.start()
        flow[...] += back[:, 128:256]

        gx = tn(xs[j], pcot[...])
        gy = tn(gated[j], ycat[...])
        grad[j, :, :, 0:512] = gx.astype(BF16).reshape(GROUP, 16, 512)
        packed = jnp.where(low_half, gy[0:128, 128:256], gy[128:256, 128:256])
        grad[j, :, :, 512:640] = packed.astype(BF16).reshape(GROUP, 16, 128)
        grad[j, :, :, 640:768] = gy[0:128, 0:128].astype(BF16).reshape(GROUP, 16, 128)
        grad[j, :, :, 768:896] = gy[128:256, 0:128].astype(BF16).reshape(GROUP, 16, 128)

        for k in range(LAYERS - j):
            stages[k](j + k)

        third.wait()
        edge = has_after * past_in[j, :, 0:head, :].astype(F32)
        moved = edge[:, 0:d, :]
        if d < ROWS:
            moved = jnp.concatenate([past.astype(F32)[:, d:, :], moved], 1)
        flow[...] += moved.reshape(N, 128)

    signal_cot[...] = flow[:, 0:RES].astype(BF16).reshape(SEQ, ROWS, RES)
    for tail in range(1, LAYERS + 1):
        for k in range(tail, LAYERS + 1):
            if k - tail < LAYERS:
                stages[k](k - tail)

    for j in range(LAYERS):
        red_wait(red_send.at[0, j], rs_in.at[j])
        if nz > 1:
            red_wait(red_send.at[1, j], part_in.at[j])
            red_wait(red_send.at[3, j], final.at[j, 0, pl.ds(0, nz - 1)])
        if ny > 1:
            red_wait(red_send.at[2, j], line_in.at[j, pl.ds(0, ny - 1)])
        red_wait(red_send.at[4, j], final.at[j, pl.ds(0, GROUP - 1)])


def on_device(ny, nz, signal, skip_grad, stream_grad, w_past, w_now, w_res, w_skip):
    tz = TILES // nz
    scale = 1.0 / math.sqrt(N * 8 * ny * nz)
    vmem = pl.BlockSpec(memory_space=pltpu.VMEM)
    shapes = (
        (SEQ, ROWS, SKIP), (SEQ, ROWS, RES), (SEQ, ROWS, RES),
        (LAYERS, RES, 2 * GATE), (LAYERS, RES, 2 * GATE), (LAYERS, GATE, RES), (LAYERS, GATE, SKIP),
    )
    bf = functools.partial(pltpu.VMEM, dtype=BF16)
    fp = functools.partial(pltpu.VMEM, dtype=F32)
    return pl.pallas_call(
        functools.partial(kernel, ny, nz, scale),
        out_shape=tuple(jax.ShapeDtypeStruct(s, BF16) for s in shapes),
        in_specs=[vmem] * 7,
        out_specs=tuple([vmem] * 7),
        scratch_shapes=[
            bf((LAYERS, 128, 512)),
            bf((LAYERS, 256, 512)),
            bf((LAYERS, 256, 256)),
            bf((LAYERS, 256, 256)),
            fp((LAYERS, SEQ, 256, 128)),
            bf((LAYERS, N, 128)),
            fp((N, 512)),
            bf((N, 256)),
            bf((LAYERS, N, 256)),
            fp((LAYERS, N, 256)),
            fp((LAYERS, N, 256)),
            fp((N, 128)),
            fp((N, 128)),
            fp((N, 256)),
            bf((N, 256)),
            bf((N, 512)),
            bf((SEQ, ROWS, RES)),
            bf((SEQ, ROWS, 128)),
            bf((SEQ, ROWS, 128)),
            bf((LAYERS, SEQ, ROWS, 128)),
            bf((LAYERS, SEQ, ROWS, 128)),
            bf((LAYERS, GROUP, 16, 896)),
            bf((LAYERS, GROUP - 1, 16, 896)),
            bf((LAYERS, nz, tz, 16, 128)),
            bf((LAYERS, max(nz - 1, 1), tz, 16, 128)),
            bf((LAYERS, ny, tz, 16, 128)),
            bf((LAYERS, GROUP, nz, tz, 16, 128)),
            pltpu.SemaphoreType.DMA((7,)),
            pltpu.SemaphoreType.DMA((7,)),
            pltpu.SemaphoreType.DMA((5, LAYERS)),
            pltpu.SemaphoreType.DMA((5, LAYERS)),
        ],
        compiler_params=pltpu.CompilerParams(
            collective_id=0, has_side_effects=True, vmem_limit_bytes=60 * 1024 * 1024
        ),
    )(signal, skip_grad, stream_grad, w_past, w_now, w_res, w_skip)


def solution(mesh):
    blocks = mesh.shape["tm"]
    ny, nz = {128: (8, 8), 4: (1, 2), 8: (2, 2)}[blocks]
    split = P("batch", "tm", None)
    return jax.shard_map(
        functools.partial(on_device, ny, nz),
        mesh=mesh,
        in_specs=(split, split, split, P(), P(), P(), P()),
        out_specs=(split, split, split, P(), P(), P(), P()),
        check_vma=False,
    )
```

time: 408 us -> 93.6 us (0.23)
  waiting for transfers between devices: 333 us -> 0 us
  Pallas kernels: 0 us -> 80.7 us
  starting transfers between devices: 26.9 us -> 0 us
  matrix products: 19.7 us -> 0 us
  between operations: 14.6 us -> 0.67 us
  local copies, waits for them, and re-layouts: 6.03 us -> 11.9 us
  other arithmetic: 5.5 us -> 0 us
    psum x1 -> x0, waiting for transfers between devices: 307 us -> none  [on_device(): totals = lax.psum(stacked, ('tm', 'batch'))]
    pallas_call x0 -> x1, Pallas kernels: none -> 80.7 us  [on_device(): pl.pallas_call(functools.partial(kernel, ny, nz, scale), out_shape=tuple(...]
    ppermute x10 -> x0, starting transfers between devices: 26.8 us -> none  [from_behind(): return lax.ppermute(block, axis, route)]
    ppermute x10 -> x0, waiting for transfers between devices: 26.5 us -> none  [from_behind(): return lax.ppermute(block, axis, route)]
    dot_general x60 -> x0, matrix products: 19.7 us -> none  [the longest x20 8.41 us: product_transposed(): jnp.einsum('stc,rc->str', left, right, preferred_element_type=jnp.float32)]
    convert_element_type x7 -> x0, other arithmetic: 5.5 us -> none  [the longest x3 4.62 us: on_device(): finals = tuple(((total * scale).astype(jnp.bfloat16) for total in totals))]
    pallas_call x0 -> x3, local copies, waits for them, and re-layouts: none -> 4.12 us  [on_device(): pl.pallas_call(functools.partial(kernel, ny, nz, scale), out_shape=tuple(...]
  transfers between devices with their start and end apart: 11 -> 0, of which waited for: 10 -> 0; matrix products, arithmetic and copies ran while one was open for 2% -> 0% of each run, Pallas kernels for 0% -> 0%
where the time goes in v1:
time: 93.6 us; the launch traced here: 93.2 us
  Pallas kernels  80.7 us (86%)
  local copies, waits for them, and re-layouts  11.9 us (13%)
    pallas_call x1, Pallas kernels, on_device(): pl.pallas_call(functools.partial(kernel, ny, nz, scale), out_shape=tuple(...  80.7 us
    unnamed x19, local copies, waits for them, and re-layouts  7.78 us
    pallas_call x3, local copies, waits for them, and re-layouts, on_device(): pl.pallas_call(functools.partial(kernel, ny, nz, scale), out_shape=tuple(...  4.12 us

profile of v1, /device:TPU:1, one launch (start us, length us, event | category | flops | bytes accessed | tf_op | source)
XLA Modules:
  0.0 93.2 jit_solution(10282009738854903155)
XLA Ops:
  0.6 0.0 copy-start.4
  0.6 1.6 %copy.14.signal = bf16[4,128,64]{2,1,0:T(8,128)(2,1)} copy(bf16[4,128,64]{1,2,0:T(8,128)(2,1)} %param.7) | data formatting | bytes 131072 | tf_op args[0]
  2.3 1.6 %copy.15.stream_grad = bf16[4,128,64]{2,1,0:T(8,128)(2,1)} copy(bf16[4,128,64]{1,2,0:T(8,128)(2,1)} %param.9) | data formatting | bytes 131072 | tf_op args[2]
  3.9 0.0 copy-done.4
  3.9 0.9 copy.16.w_res
  4.8 80.7 %shard_map.126 = (bf16[4,128,128]{2,1,0:T(8,128)(2,1)}, bf16[4,128,64]{2,1,0:T(8,128)(2,1)}, bf16[4,128,64]{2,1,0:T(8,128)(2,1)}, bf16[5,64,512]{2,1,0:T(8,128)(...) custom-call(bf16[4,128,64]{2,1,0:T(8,128)(2,1)} %copy.14.signal, ...), custom_call_target="tpu_custom_call" | custom-call | tf_op jit(solution)/shard_map/pallas_call | solution.py:304
  85.4 0.0 copy-start.3
  85.5 1.7 %copy.17 = bf16[4,128,64]{1,2,0:T(8,128)(2,1)} copy(bf16[4,128,64]{2,1,0:T(8,128)(2,1)} %get-tuple-element.8) | data formatting | bytes 131072 | tf_op jit(solution)/shard_map/pallas_call | solution.py:304
  87.1 1.6 %copy.18 = bf16[4,128,64]{1,2,0:T(8,128)(2,1)} copy(bf16[4,128,64]{2,1,0:T(8,128)(2,1)} %get-tuple-element.9) | data formatting | bytes 131072 | tf_op jit(solution)/shard_map/pallas_call | solution.py:304
  88.7 0.0 copy-done.3
  88.7 0.0 copy-start.5
  88.7 0.0 copy-start.2
  88.7 0.8 copy.19
  89.6 0.1 copy-done.5
  89.6 0.7 copy.24
  90.3 0.0 copy-done.2
  90.3 0.0 copy-start.1
  90.3 0.7 copy.25
  91.0 0.4 copy-done.1
  91.4 0.0 copy-start
  91.4 0.7 copy.26
  92.1 0.4 copy-done
  92.5 0.7 copy.27
Async XLA Ops:
  0.6 3.2 %copy-start.4 = (bf16[5,256,64]{1,2,0:T(8,128)(2,1)S(1)}, bf16[5,256,64]{1,2,0:T(8,128)(2,1)}, u32[]{:S(2)}) copy-start(bf16[5,256,64]{1,2,0:T(8,128)(2,1)} %param.12) | copy-start | bytes 491524
  85.4 3.3 %copy-start.3 = (bf16[5,256,64]{2,1,0:T(8,128)(2,1)S(1)}, bf16[5,256,64]{2,1,0:T(8,128)(2,1)}, u32[]{:S(2)}) copy-start(bf16[5,256,64]{2,1,0:T(8,128)(2,1)} %get-tuple-element.12) | copy-start | bytes 491524
  88.7 0.9 copy-start.5
  88.7 1.6 %copy-start.2 = (bf16[5,64,512]{2,1,0:T(8,128)(2,1)S(1)}, bf16[5,64,512]{2,1,0:T(8,128)(2,1)}, u32[]{:S(2)}) copy-start(bf16[5,64,512]{2,1,0:T(8,128)(2,1)} %get-tuple-element.24) | copy-start | bytes 983044
  90.3 1.1 %copy-start.1 = (bf16[5,64,512]{2,1,0:T(8,128)(2,1)S(1)}, bf16[5,64,512]{2,1,0:T(8,128)(2,1)}, u32[]{:S(2)}) copy-start(bf16[5,64,512]{2,1,0:T(8,128)(2,1)} %get-tuple-element.25) | copy-start | bytes 983044
  91.4 1.1 %copy-start = (bf16[5,256,128]{2,1,0:T(8,128)(2,1)S(1)}, bf16[5,256,128]{2,1,0:T(8,128)(2,1)}, u32[]{:S(2)}) copy-start(bf16[5,256,128]{2,1,0:T(8,128)(2,1)} %get-tuple-element.27) | copy-start | bytes 983044

commit v2 on v1

v2 whole, which is shorter than its diff:
```python
import functools
import math

import jax
import jax.numpy as jnp
from jax import lax
from jax.experimental import pallas as pl
from jax.experimental.pallas import tpu as pltpu
from jax.sharding import PartitionSpec as P

MESH = pl.DeviceIdType.MESH
F32 = jnp.float32
BF16 = jnp.bfloat16

RES = 64
GATE = 256
SKIP = 128
LAYERS = 5
SEQ = 4
ROWS = 128
N = SEQ * ROWS
DIL = (8, 16, 32, 64, 128)
LOW = (16, 32, 64, 128, 128)
CHUNK = 32
NX = 4
TILES = 8
WIRE = 7


def nn(left, right):
    return jnp.dot(left, right, preferred_element_type=F32)


def nt(left, right):
    return lax.dot_general(left, right, (((1,), (1,)), ((), ())), preferred_element_type=F32)


def tn(left, right):
    return lax.dot_general(left, right, (((0,), (0,)), ((), ())), preferred_element_type=F32)


def kernel(
    ny, nz, scale,
    signal, skip_grad, stream_grad, w_past, w_now, w_res, w_skip,
    skip_out, stream_out, signal_cot, g_past, g_now, g_res, g_skip,
    sig, sgrad, wres, skipg, skip_st, stream_st, cot_st, past_st, now_st, res_st, gskip_st,
    wx, wb, wf, wg, h2, xs, pre, gat_ext, gated, dfilt, dgate, skip_acc, flow, gcot, flow_b, pcot,
    sig_in, h4_out, h4_in, past_f, past_out, past_in,
    grad, pair_in, half, ring_in, part, part_in, line_in, final,
    load_sem, out_sem, halo_send, halo_recv, red_send, red_recv,
):
    tm = lax.axis_index("tm")
    batch = lax.axis_index("batch")
    blocks = ny * nz * 2
    x_lo = tm % 2
    core = batch % 2
    xi = (batch // 2) * 2 + x_lo
    zi = (tm // 2) % nz
    yi = tm // (2 * nz)
    ei = core * NX + xi
    tz = TILES // nz

    after = {"tm": (tm + 1) % blocks, "batch": batch}
    before = {"tm": (tm + blocks - 1) % blocks, "batch": batch}
    sibling = {"tm": tm, "batch": batch + 1 - 2 * core}
    x_peers = []
    for r in range(1, NX):
        x = (xi + r) % NX
        x_peers.append((x, {"tm": tm - x_lo + x % 2, "batch": (x // 2) * 2 + core}))
    z_peers = []
    for r in range(1, nz):
        z = (zi + r) % nz
        z_peers.append((z, {"tm": (yi * nz + z) * 2 + x_lo, "batch": batch}))
    y_peers = []
    for r in range(1, ny):
        y = (yi + r) % ny
        y_peers.append((y, {"tm": (y * nz + zi) * 2 + x_lo, "batch": batch}))

    barrier = pltpu.get_barrier_semaphore()
    partners = [before, after, sibling] + [peer for _, peer in x_peers + z_peers + y_peers]
    for partner in partners:
        pl.semaphore_signal(barrier, inc=1, device_id=partner, device_id_type=MESH)

    loads = []

    def load(src, dst):
        copy = pltpu.make_async_copy(src, dst, load_sem.at[len(loads)])
        copy.start()
        loads.append(copy)

    load(signal, sig)
    load(w_res, wres)
    load(w_past, wx.at[:, pl.ds(0, 64), :])
    load(w_now, wx.at[:, pl.ds(64, 64), :])
    load(w_skip, wf.at[:, :, pl.ds(0, 128)])
    load(w_skip, wg.at[:, :, pl.ds(0, 128)])
    load(stream_grad, sgrad)
    load(skip_grad, skipg)
    load(w_past, wb.at[:, pl.ds(0, 64), :])
    load(w_past, wb.at[:, pl.ds(64, 64), :])
    load(w_now, wb.at[:, pl.ds(128, 64), :])
    load(w_now, wb.at[:, pl.ds(192, 64), :])

    pl.semaphore_wait(barrier, len(partners))

    def halo_copy(which, src, dst, target):
        return pltpu.make_async_remote_copy(
            src_ref=src, dst_ref=dst, send_sem=halo_send.at[which], recv_sem=halo_recv.at[which],
            device_id=target, device_id_type=MESH,
        )

    first = halo_copy(5, signal, sig_in, after)
    first.start()

    twice = (
        lax.broadcasted_iota(jnp.int32, (RES, 128), 1) % RES
        == lax.broadcasted_iota(jnp.int32, (RES, 128), 0)
    ).astype(F32).astype(BF16)
    once = (
        lax.broadcasted_iota(jnp.int32, (RES, 128), 1)
        == lax.broadcasted_iota(jnp.int32, (RES, 128), 0)
    ).astype(F32).astype(BF16)
    low_half = lax.broadcasted_iota(jnp.int32, (1, 128), 1) < RES
    has_before = jnp.where(tm > 0, 1.0, 0.0).astype(F32)
    has_after = jnp.where(tm < blocks - 1, 1.0, 0.0).astype(F32)
    skip_acc[...] = jnp.zeros_like(skip_acc)
    loads[0].wait()
    for s in range(SEQ):
        h2[0, s, 128:256, :] = tn(sig[s], twice)
    loads[1].wait()
    for j in range(LAYERS):
        both = tn(wres[j], twice)
        wf[j, :, 128:256] = both.astype(BF16)
        wg[j, :, 128:256] = jnp.where(low_half, both, 0.0).astype(BF16)
    for copy in loads[2:]:
        copy.wait()
    for s in range(SEQ):
        flow[s] = tn(sgrad[s], twice)
    first.wait()
    for s in range(SEQ):
        h2[0, s, 0:128, :] = has_before * tn(sig_in[s], twice)

    def gates(j, lo, hi):
        own = lo == 128
        span = hi - lo
        count = SEQ * span
        d = DIL[j]
        x = jnp.where(low_half, h2[j, :, lo - d : hi - d, :], h2[j, :, lo:hi, :])
        x = x.reshape(count, 128).astype(BF16)
        if own:
            xs[j] = x
        pre[0:count, :] = nn(x, wx[j])

        def step(i, carry):
            for u in range(2):
                rows = pl.ds(pl.multiple_of(i * (2 * CHUNK) + u * CHUNK, CHUNK), CHUNK)
                t = jnp.tanh(pre[rows, 0:GATE])
                s = 0.5 * jnp.tanh(0.5 * pre[rows, GATE : 2 * GATE]) + 0.5
                ts = t * s
                if own:
                    gated[j, rows, :] = ts.astype(BF16)
                    dfilt[j, rows, :] = s * (1.0 - t * t)
                    dgate[j, rows, :] = ts * (1.0 - s)
                else:
                    gat_ext[rows, :] = ts.astype(BF16)
            return carry

        lax.fori_loop(0, count // (2 * CHUNK), step, 0)

    def advance(j, lo, hi):
        own = lo == 128
        span = hi - lo
        count = SEQ * span
        y = nn(gated[j] if own else gat_ext[0:count, :], wf[j])
        if own:
            skip_acc[...] += y[:, 0:128]
        new = h2[j, :, lo:hi, :].reshape(count, 128) + y[:, 128:256]
        new = new.astype(BF16)
        if j + 1 < LAYERS:
            h2[j + 1, :, lo:hi, :] = new.astype(F32).reshape(SEQ, span, 128)
        return new

    for j in range(4):
        if LOW[j] < 128:
            gates(j, LOW[j], 128)
            advance(j, LOW[j], 128)
        gates(j, 128, 256)
        new = advance(j, 128, 256)
    h4_out[...] = new.reshape(SEQ, ROWS, 128)
    second = halo_copy(6, h4_out, h4_in, after)
    second.start()

    def cotangent(j, a, b):
        count = SEQ * (b - a)
        fb = flow[:, a:b, :].astype(BF16)
        flow_b[j, :, a:b, :] = fb
        left = jnp.concatenate([skipg[:, a:b, :], fb], 2).reshape(count, 256)
        gcot[0:count, :] = nt(left, wg[j])

    def back(j, a, b):
        span = b - a
        count = SEQ * span
        size = CHUNK if span % CHUNK == 0 else 16
        per = span // size

        def step(i, carry):
            s = i // per
            here = pl.ds(pl.multiple_of(i * size, 16), size)
            rows = pl.ds(pl.multiple_of(a + (i % per) * size, 16), size)
            flat = pl.ds(pl.multiple_of(s * ROWS + a + (i % per) * size, 16), size)
            gc = gcot[here, :]
            pcot[j, s, rows, 0:GATE] = (gc * dfilt[j, flat, :]).astype(BF16)
            pcot[j, s, rows, GATE : 2 * GATE] = (gc * dgate[j, flat, :]).astype(BF16)
            return carry

        lax.fori_loop(0, SEQ * per, step, 0)
        both = nt(pcot[j, :, a:b, :].reshape(count, 2 * GATE), wb[j])
        past = both[:, 0:128].astype(BF16).reshape(SEQ, span, 128)
        past_out[j, :, a:b, :] = past
        past_f[j, :, a:b, :] = past.astype(F32)
        flow[:, a:b, :] += both[:, 128:256].reshape(SEQ, span, 128)

    def head_copy(j):
        rows = pl.ds(0, max(DIL[j], 16))
        return halo_copy(j, past_out.at[j, :, rows, :], past_in.at[j, :, rows, :], before)

    def move(j, a, b):
        d = DIL[j]
        lo, hi = a + d, b + d
        pieces = []
        if lo < ROWS:
            pieces.append(past_f[j, :, lo : min(hi, ROWS), :])
        if hi > ROWS:
            edge = past_in[j, :, 0 : max(d, 16), :].astype(F32)
            pieces.append(has_after * edge[:, max(lo - ROWS, 0) : hi - ROWS, :])
        flow[:, a:b, :] += pieces[0] if len(pieces) == 1 else jnp.concatenate(pieces, 1)

    def weight_sums(j):
        gx = tn(xs[j], pcot[j].reshape(N, 2 * GATE))
        right = jnp.concatenate([skipg[...], flow_b[j]], 2).reshape(N, 256)
        gy = tn(gated[j], right)
        grad[j, :, :, 0:512] = gx.astype(BF16).reshape(2 * NX, 16, 512)
        packed = jnp.where(low_half, gy[0:128, 128:256], gy[128:256, 128:256]).T
        grad[j, :, :, 512:640] = packed.astype(BF16).reshape(2 * NX, 16, 128)
        grad[j, :, :, 640:768] = gy[0:128, 0:128].astype(BF16).reshape(2 * NX, 16, 128)
        grad[j, :, :, 768:896] = gy[128:256, 0:128].astype(BF16).reshape(2 * NX, 16, 128)

    def red_copy(stage, j, src, dst, target):
        pltpu.make_async_remote_copy(
            src_ref=src, dst_ref=dst, send_sem=red_send.at[stage, j], recv_sem=red_recv.at[stage, j],
            device_id=target, device_id_type=MESH,
        ).start()

    def red_wait(sem, ref):
        pltpu.make_async_copy(ref, ref, sem).wait()

    mine = pl.ds(core * NX, NX)
    other = pl.ds((1 - core) * NX, NX)

    def scatter_core(j):
        red_copy(0, j, grad.at[j, other], pair_in.at[j], sibling)

    def scatter_x(j):
        red_wait(red_recv.at[0, j], pair_in.at[j])
        half[j] = (grad[j, mine].astype(F32) + pair_in[j].astype(F32)).astype(BF16)
        for r, (x, peer) in enumerate(x_peers):
            red_copy(1, j, half.at[j, x], ring_in.at[j, r], peer)

    def scatter_z(j):
        red_wait(red_recv.at[1, j], ring_in.at[j])
        total = half[j, xi].astype(F32)
        for r in range(NX - 1):
            total += ring_in[j, r].astype(F32)
        for k in range(WIRE):
            part[j, k // tz, k % tz] = total[:, 128 * k : 128 * k + 128].astype(BF16)
        for k in range(WIRE, TILES):
            part[j, k // tz, k % tz] = jnp.zeros((16, 128), BF16)
        for r, (z, peer) in enumerate(z_peers):
            red_copy(2, j, part.at[j, z], part_in.at[j, r], peer)

    def across_y(j):
        if nz > 1:
            red_wait(red_recv.at[2, j], part_in.at[j])
        total = part[j, zi].astype(F32)
        for r in range(nz - 1):
            total += part_in[j, r].astype(F32)
        line_in[j, yi] = total.astype(BF16)
        for _, peer in y_peers:
            red_copy(3, j, line_in.at[j, yi], line_in.at[j, yi], peer)

    def gather_z(j):
        if ny > 1:
            red_wait(red_recv.at[3, j], line_in.at[j, pl.ds(0, ny - 1)])
        total = line_in[j, 0].astype(F32)
        for r in range(1, ny):
            total += line_in[j, r].astype(F32)
        final[j, ei, zi] = (total * scale).astype(BF16)
        for _, peer in z_peers:
            red_copy(4, j, final.at[j, ei, zi], final.at[j, ei, zi], peer)

    def gather_x(j):
        if nz > 1:
            red_wait(red_recv.at[4, j], final.at[j, 0, pl.ds(0, nz - 1)])
        for _, peer in x_peers:
            red_copy(5, j, final.at[j, ei], final.at[j, ei], peer)

    def gather_core(j):
        red_wait(red_recv.at[5, j], final.at[j, pl.ds(0, NX - 1)])
        red_copy(6, j, final.at[j, mine], final.at[j, mine], sibling)

    def store(which, src, dst):
        pltpu.make_async_copy(src, dst, out_sem.at[which]).start()

    def finish(j):
        red_wait(red_recv.at[6, j], final.at[j, pl.ds(0, NX)])
        tile = [final[j, :, k // tz, k % tz].reshape(128, 128) for k in range(WIRE)]
        for k in range(4):
            past_st[j, :, 128 * k : 128 * k + 128] = tile[k][0:64]
            now_st[j, :, 128 * k : 128 * k + 128] = tile[k][64:128]
        res_st[j, :, 0:128] = tile[4][0:64]
        res_st[j, :, 128:256] = tile[4][64:128]
        gskip_st[j, 0:128, :] = tile[5]
        gskip_st[j, 128:256, :] = tile[6]
        store(3, past_st.at[j], g_past.at[j])
        store(4, now_st.at[j], g_now.at[j])
        store(5, res_st.at[j], g_res.at[j])
        store(6, gskip_st.at[j], g_skip.at[j])

    stages = (
        scatter_core, scatter_x, scatter_z, across_y, gather_z, gather_x, gather_core, finish
    )

    def turn(*work):
        for k, j in work:
            stages[k](j)

    cotangent(4, 0, ROWS)
    second.wait()
    h2[4, :, 0:128, :] = has_before * h4_in[...].astype(F32)
    gates(4, 128, 256)
    heads = [head_copy(j) for j in range(LAYERS)]
    back(4, 0, ROWS)
    heads[4].start()
    new = advance(4, 128, 256)
    for s in range(SEQ):
        stream_st[s] = nt(once, new[s * ROWS : (s + 1) * ROWS]).astype(BF16)
    skip_st[...] = skip_acc[...].astype(BF16).reshape(SEQ, ROWS, SKIP)
    store(0, skip_st, skip_out)
    store(1, stream_st, stream_out)
    weight_sums(4)
    turn((0, 4))

    heads[4].wait()
    move(4, 0, ROWS)
    cotangent(3, 0, ROWS)
    back(3, 0, ROWS)
    heads[3].start()
    for j in (3, 2, 1):
        d = DIL[j]
        move(j, 0, d)
        cotangent(j - 1, 0, d)
        back(j - 1, 0, d)
        heads[j - 1].start()
    weight_sums(3)
    turn((0, 3), (1, 4))
    during = {
        3: ((0, 2), (1, 3)),
        2: ((0, 1), (1, 2), (2, 4)),
        1: ((0, 0), (1, 1), (1, 0), (2, 3), (2, 2), (3, 4)),
    }
    for j in (3, 2, 1):
        d = DIL[j]
        heads[j].wait()
        move(j, d, ROWS)
        cotangent(j - 1, d, ROWS)
        back(j - 1, d, ROWS)
        weight_sums(j - 1)
        turn(*during[j])
    heads[0].wait()
    move(0, 0, ROWS)
    for s in range(SEQ):
        cot_st[s] = nt(once, flow[s].astype(BF16)).astype(BF16)
    store(2, cot_st, signal_cot)
    for k in range(2, len(stages)):
        turn((k, 0), (k, 1))
        if k + 1 < len(stages):
            turn((k + 1, 3), (k + 1, 2))
        if k + 2 < len(stages):
            turn((k + 2, 4))

    for j in range(LAYERS):
        red_wait(red_send.at[0, j], pair_in.at[j])
        red_wait(red_send.at[1, j], ring_in.at[j])
        if nz > 1:
            red_wait(red_send.at[2, j], part_in.at[j])
            red_wait(red_send.at[4, j], final.at[j, 0, pl.ds(0, nz - 1)])
        if ny > 1:
            red_wait(red_send.at[3, j], line_in.at[j, pl.ds(0, ny - 1)])
        red_wait(red_send.at[5, j], final.at[j, pl.ds(0, NX - 1)])
        red_wait(red_send.at[6, j], final.at[j, pl.ds(0, NX)])
    staged = (skip_st, stream_st, cot_st, past_st, now_st, res_st, gskip_st)
    outs = (skip_out, stream_out, signal_cot, g_past, g_now, g_res, g_skip)
    for which in range(7):
        pltpu.make_async_copy(staged[which], outs[which], out_sem.at[which]).wait()


def relay(*refs):
    ins, outs, held, in_sem, out_sem = refs[:7], refs[7:14], refs[14:21], refs[21], refs[22]
    loads = [pltpu.make_async_copy(ins[i], held[i], in_sem.at[i]) for i in range(7)]
    stores = [pltpu.make_async_copy(held[i], outs[i], out_sem.at[i]) for i in range(7)]
    for copy in loads:
        copy.start()
    for i in range(7):
        loads[i].wait()
        stores[i].start()
    for copy in stores:
        copy.wait()


def on_device(ny, nz, signal, skip_grad, stream_grad, w_past, w_now, w_res, w_skip):
    tz = TILES // nz
    scale = 1.0 / math.sqrt(N * 8 * ny * nz)
    shapes = (
        (SEQ, ROWS, SKIP), (SEQ, RES, ROWS), (SEQ, RES, ROWS),
        (LAYERS, RES, 2 * GATE), (LAYERS, RES, 2 * GATE), (LAYERS, RES, GATE), (LAYERS, GATE, SKIP),
    )
    anywhere = pl.BlockSpec(memory_space=pl.ANY)
    results = tuple(jax.ShapeDtypeStruct(s, BF16) for s in shapes)
    bf = functools.partial(pltpu.VMEM, dtype=BF16)
    fp = functools.partial(pltpu.VMEM, dtype=F32)
    outs = pl.pallas_call(
        functools.partial(kernel, ny, nz, scale),
        out_shape=results,
        in_specs=[anywhere] * 7,
        out_specs=(anywhere,) * 7,
        scratch_shapes=[
            bf((SEQ, RES, ROWS)),
            bf((SEQ, RES, ROWS)),
            bf((LAYERS, RES, GATE)),
            bf((SEQ, ROWS, SKIP)),
            *[bf(s) for s in shapes],
            bf((LAYERS, 128, 512)),
            bf((LAYERS, 256, 512)),
            bf((LAYERS, 256, 256)),
            bf((LAYERS, 256, 256)),
            fp((LAYERS, SEQ, 256, 128)),
            bf((LAYERS, N, 128)),
            fp((N, 512)),
            bf((N, 256)),
            bf((LAYERS, N, 256)),
            fp((LAYERS, N, 256)),
            fp((LAYERS, N, 256)),
            fp((N, 128)),
            fp((SEQ, ROWS, 128)),
            fp((N, 256)),
            bf((LAYERS, SEQ, ROWS, 128)),
            bf((LAYERS, SEQ, ROWS, 512)),
            bf((SEQ, RES, ROWS)),
            bf((SEQ, ROWS, 128)),
            bf((SEQ, ROWS, 128)),
            fp((LAYERS, SEQ, ROWS, 128)),
            bf((LAYERS, SEQ, ROWS, 128)),
            bf((LAYERS, SEQ, ROWS, 128)),
            bf((LAYERS, 2 * NX, 16, 896)),
            bf((LAYERS, NX, 16, 896)),
            bf((LAYERS, NX, 16, 896)),
            bf((LAYERS, NX - 1, 16, 896)),
            bf((LAYERS, nz, tz, 16, 128)),
            bf((LAYERS, max(nz - 1, 1), tz, 16, 128)),
            bf((LAYERS, ny, tz, 16, 128)),
            bf((LAYERS, 2 * NX, nz, tz, 16, 128)),
            pltpu.SemaphoreType.DMA((12,)),
            pltpu.SemaphoreType.DMA((7,)),
            pltpu.SemaphoreType.DMA((7,)),
            pltpu.SemaphoreType.DMA((7,)),
            pltpu.SemaphoreType.DMA((7, LAYERS)),
            pltpu.SemaphoreType.DMA((7, LAYERS)),
        ],
        compiler_params=pltpu.CompilerParams(
            collective_id=0, has_side_effects=True, vmem_limit_bytes=60 * 1024 * 1024
        ),
    )(
        jnp.swapaxes(signal, 1, 2), skip_grad, jnp.swapaxes(stream_grad, 1, 2),
        w_past, w_now, jnp.swapaxes(w_res, 1, 2), w_skip,
    )
    outs = pl.pallas_call(
        relay,
        out_shape=results,
        in_specs=[anywhere] * 7,
        out_specs=(anywhere,) * 7,
        scratch_shapes=[*[bf(s) for s in shapes]] + [pltpu.SemaphoreType.DMA((7,))] * 2,
    )(*outs)
    skip, stream, cot, g_past, g_now, g_res, g_skip = outs
    return (
        skip, jnp.swapaxes(stream, 1, 2), jnp.swapaxes(cot, 1, 2),
        g_past, g_now, jnp.swapaxes(g_res, 1, 2), g_skip,
    )


def solution(mesh):
    blocks = mesh.shape["tm"]
    ny, nz = {128: (8, 8), 4: (1, 2), 8: (2, 2)}[blocks]
    split = P("batch", "tm", None)
    return jax.shard_map(
        functools.partial(on_device, ny, nz),
        mesh=mesh,
        in_specs=(split, split, split, P(), P(), P(), P()),
        out_specs=(split, split, split, P(), P(), P(), P()),
        check_vma=False,
    )
```

time: 93.6 us -> 75.9 us (0.81)
  local copies, waits for them, and re-layouts: 11.9 us -> 0 us
  Pallas kernels: 80.7 us -> 75.1 us
    unnamed x19 -> x0, local copies, waits for them, and re-layouts: 7.78 us -> none
    pallas_call x1 -> x2, Pallas kernels: 80.7 us -> 75.1 us  [the longest x1 72.9 us: on_device(): pl.pallas_call(functools.partial(kernel, ny, nz, scale), out_shape=result...]
    pallas_call x3 -> x0, local copies, waits for them, and re-layouts: 4.12 us -> none  [on_device(): pl.pallas_call(functools.partial(kernel, ny, nz, scale), out_shape=tuple(...]
where the time goes in v2:
time: 75.9 us; the launch traced here: 75.8 us
  Pallas kernels  75.1 us (99%)
    pallas_call x1, Pallas kernels, on_device(): pl.pallas_call(functools.partial(kernel, ny, nz, scale), out_shape=result...  72.9 us
    pallas_call x1, Pallas kernels, on_device(): pl.pallas_call(relay, out_shape=results, in_specs=[anywhere] * 7, out_spe...  2.23 us

profile of v2, /device:TPU:1, one launch (start us, length us, event | category | flops | bytes accessed | tf_op | source)
XLA Modules:
  0.0 75.8 jit_solution(13295799775022894626)
XLA Ops:
  0.6 72.9 %shard_map.126 = (bf16[4,128,128]{2,1,0:T(8,128)(2,1)}, bf16[4,64,128]{2,1,0:T(8,128)(2,1)}, bf16[4,64,128]{2,1,0:T(8,128)(2,1)}, bf16[5,64,512]{2,1,0:T(8,128)(...) custom-call(bf16[4,64,128]{2,1,0:T(8,128)(2,1)} %bitcast.7, ...), custom_call_target="tpu_custom_call" | custom-call | tf_op jit(solution)/shard_map/pallas_call | solution.py:431
  73.6 2.2 %shard_map.127 = (bf16[4,128,128]{2,1,0:T(8,128)(2,1)}, bf16[4,64,128]{2,1,0:T(8,128)(2,1)}, bf16[4,64,128]{2,1,0:T(8,128)(2,1)}, bf16[5,64,512]{2,1,0:T(8,128)(...) custom-call(bf16[4,128,128]{2,1,0:T(8,128)(2,1)} %get-tuple-element.21.refs_0_, ...), custom_call_target="tpu_custom_call" | custom-call | tf_op jit(solution)/shard_map/pallas_call | solution.py:486

commit v3 on v2

--- a/solution.py
+++ b/solution.py
@@ -39,15 +39,19 @@
     return lax.dot_general(left, right, (((0,), (0,)), ((), ())), preferred_element_type=F32)
 
 
+def far_first(n):
+    return sorted(range(1, n), key=lambda r: -min(r, n - r))
+
+
 def kernel(
     ny, nz, scale,
     signal, skip_grad, stream_grad, w_past, w_now, w_res, w_skip,
-    skip_out, stream_out, signal_cot, g_past, g_now, g_res, g_skip,
-    sig, sgrad, wres, skipg, skip_st, stream_st, cot_st, past_st, now_st, res_st, gskip_st,
-    wx, wb, wf, wg, h2, xs, pre, gat_ext, gated, dfilt, dgate, skip_acc, flow, gcot, flow_b, pcot,
+    skip_st, stream_st, cot_st, past_st, now_st, res_st, gskip_st,
+    sig, sgrad, wres, skipg,
+    wx, wb, wf, wg, h2, xs, pre, gated, dfilt, dgate, skip_acc, flow, gcot, flow_b, pcot,
     sig_in, h4_out, h4_in, past_f, past_out, past_in,
     grad, pair_in, half, ring_in, part, part_in, line_in, final,
-    load_sem, out_sem, halo_send, halo_recv, red_send, red_recv,
+    load_sem, halo_send, halo_recv, red_send, red_recv,
 ):
     tm = lax.axis_index("tm")
     batch = lax.axis_index("batch")
@@ -64,15 +68,15 @@
     before = {"tm": (tm + blocks - 1) % blocks, "batch": batch}
     sibling = {"tm": tm, "batch": batch + 1 - 2 * core}
     x_peers = []
-    for r in range(1, NX):
+    for r in far_first(NX):
         x = (xi + r) % NX
         x_peers.append((x, {"tm": tm - x_lo + x % 2, "batch": (x // 2) * 2 + core}))
     z_peers = []
-    for r in range(1, nz):
+    for r in far_first(nz):
         z = (zi + r) % nz
         z_peers.append((z, {"tm": (yi * nz + z) * 2 + x_lo, "batch": batch}))
     y_peers = []
-    for r in range(1, ny):
+    for r in far_first(ny):
         y = (yi + r) % ny
         y_peers.append((y, {"tm": (y * nz + zi) * 2 + x_lo, "batch": batch}))
 
@@ -136,57 +140,54 @@
         copy.wait()
     for s in range(SEQ):
         flow[s] = tn(sgrad[s], twice)
+
+    def gates(j, lo, hi):
+        span = hi - lo
+        count = SEQ * span
+        d = DIL[j]
+        size = CHUNK if span % CHUNK == 0 else 16
+        own = max(lo, 128)
+        x = jnp.where(low_half, h2[j, :, lo - d : hi - d, :], h2[j, :, lo:hi, :]).astype(BF16)
+        xs[j, :, own - 128 : hi - 128, :] = x[:, own - lo :, :]
+        pre[0:count, :] = nn(x.reshape(count, 128), wx[j])
+
+        def step(q, carry):
+            for c in range(0, span, size):
+                rows = pl.ds(pl.multiple_of(q * span + c, 16), size)
+                t = jnp.tanh(pre[rows, 0:GATE])
+                s = 0.5 * jnp.tanh(0.5 * pre[rows, GATE : 2 * GATE]) + 0.5
+                ts = t * s
+                gated[j, q, lo + c : lo + c + size, :] = ts.astype(BF16)
+                if lo + c + size > 128:
+                    dfilt[j, q, lo + c : lo + c + size, :] = s * (1.0 - t * t)
+                    dgate[j, q, lo + c : lo + c + size, :] = ts * (1.0 - s)
+            return carry
+
+        lax.fori_loop(0, SEQ, step, 0)
+
+    def advance(j, lo, hi):
+        span = hi - lo
+        count = SEQ * span
+        own = max(lo, 128)
+        y = nn(gated[j, :, lo:hi, :].reshape(count, GATE), wf[j]).reshape(SEQ, span, 256)
+        skip_acc[:, own - 128 : hi - 128, :] += y[:, own - lo :, 0:128]
+        new = (h2[j, :, lo:hi, :] + y[:, :, 128:256]).astype(BF16)
+        if j + 1 < LAYERS:
+            h2[j + 1, :, lo:hi, :] = new.astype(F32)
+        return new
+
+    for j in range(3):
+        gates(j, LOW[j] + 128, 256)
+        advance(j, LOW[j] + 128, 256)
     first.wait()
     for s in range(SEQ):
         h2[0, s, 0:128, :] = has_before * tn(sig_in[s], twice)
-
-    def gates(j, lo, hi):
-        own = lo == 128
-        span = hi - lo
-        count = SEQ * span
-        d = DIL[j]
-        x = jnp.where(low_half, h2[j, :, lo - d : hi - d, :], h2[j, :, lo:hi, :])
-        x = x.reshape(count, 128).astype(BF16)
-        if own:
-            xs[j] = x
-        pre[0:count, :] = nn(x, wx[j])
-
-        def step(i, carry):
-            for u in range(2):
-                rows = pl.ds(pl.multiple_of(i * (2 * CHUNK) + u * CHUNK, CHUNK), CHUNK)
-                t = jnp.tanh(pre[rows, 0:GATE])
-                s = 0.5 * jnp.tanh(0.5 * pre[rows, GATE : 2 * GATE]) + 0.5
-                ts = t * s
-                if own:
-                    gated[j, rows, :] = ts.astype(BF16)
-                    dfilt[j, rows, :] = s * (1.0 - t * t)
-                    dgate[j, rows, :] = ts * (1.0 - s)
-                else:
-                    gat_ext[rows, :] = ts.astype(BF16)
-            return carry
-
-        lax.fori_loop(0, count // (2 * CHUNK), step, 0)
-
-    def advance(j, lo, hi):
-        own = lo == 128
-        span = hi - lo
-        count = SEQ * span
-        y = nn(gated[j] if own else gat_ext[0:count, :], wf[j])
-        if own:
-            skip_acc[...] += y[:, 0:128]
-        new = h2[j, :, lo:hi, :].reshape(count, 128) + y[:, 128:256]
-        new = new.astype(BF16)
-        if j + 1 < LAYERS:
-            h2[j + 1, :, lo:hi, :] = new.astype(F32).reshape(SEQ, span, 128)
-        return new
-
-    for j in range(4):
-        if LOW[j] < 128:
-            gates(j, LOW[j], 128)
-            advance(j, LOW[j], 128)
-        gates(j, 128, 256)
-        new = advance(j, 128, 256)
-    h4_out[...] = new.reshape(SEQ, ROWS, 128)
+    for j in range(3):
+        gates(j, LOW[j], LOW[j] + 128)
+        advance(j, LOW[j], LOW[j] + 128)
+    gates(3, 128, 256)
+    new = advance(3, 128, 256)
+    h4_out[...] = new
     second = halo_copy(6, h4_out, h4_in, after)
     second.start()
 
@@ -207,10 +208,10 @@
             s = i // per
             here = pl.ds(pl.multiple_of(i * size, 16), size)
             rows = pl.ds(pl.multiple_of(a + (i % per) * size, 16), size)
-            flat = pl.ds(pl.multiple_of(s * ROWS + a + (i % per) * size, 16), size)
+            held = pl.ds(pl.multiple_of(128 + a + (i % per) * size, 16), size)
             gc = gcot[here, :]
-            pcot[j, s, rows, 0:GATE] = (gc * dfilt[j, flat, :]).astype(BF16)
-            pcot[j, s, rows, GATE : 2 * GATE] = (gc * dgate[j, flat, :]).astype(BF16)
+            pcot[j, s, rows, 0:GATE] = (gc * dfilt[j, s, held, :]).astype(BF16)
+            pcot[j, s, rows, GATE : 2 * GATE] = (gc * dgate[j, s, held, :]).astype(BF16)
             return carry
 
         lax.fori_loop(0, SEQ * per, step, 0)
@@ -236,9 +237,9 @@
         flow[:, a:b, :] += pieces[0] if len(pieces) == 1 else jnp.concatenate(pieces, 1)
 
     def weight_sums(j):
-        gx = tn(xs[j], pcot[j].reshape(N, 2 * GATE))
+        gx = tn(xs[j].reshape(N, 128), pcot[j].reshape(N, 2 * GATE))
         right = jnp.concatenate([skipg[...], flow_b[j]], 2).reshape(N, 256)
-        gy = tn(gated[j], right)
+        gy = tn(gated[j, :, 128:256, :].reshape(N, GATE), right)
         grad[j, :, :, 0:512] = gx.astype(BF16).reshape(2 * NX, 16, 512)
         packed = jnp.where(low_half, gy[0:128, 128:256], gy[128:256, 128:256]).T
         grad[j, :, :, 512:640] = packed.astype(BF16).reshape(2 * NX, 16, 128)
@@ -308,9 +309,6 @@
         red_wait(red_recv.at[5, j], final.at[j, pl.ds(0, NX - 1)])
         red_copy(6, j, final.at[j, mine], final.at[j, mine], sibling)
 
-    def store(which, src, dst):
-        pltpu.make_async_copy(src, dst, out_sem.at[which]).start()
-
     def finish(j):
         red_wait(red_recv.at[6, j], final.at[j, pl.ds(0, NX)])
         tile = [final[j, :, k // tz, k % tz].reshape(128, 128) for k in range(WIRE)]
@@ -321,10 +319,6 @@
         res_st[j, :, 128:256] = tile[4][64:128]
         gskip_st[j, 0:128, :] = tile[5]
         gskip_st[j, 128:256, :] = tile[6]
-        store(3, past_st.at[j], g_past.at[j])
-        store(4, now_st.at[j], g_now.at[j])
-        store(5, res_st.at[j], g_res.at[j])
-        store(6, gskip_st.at[j], g_skip.at[j])
 
     stages = (
         scatter_core, scatter_x, scatter_z, across_y, gather_z, gather_x, gather_core, finish
@@ -343,18 +337,18 @@
     heads[4].start()
     new = advance(4, 128, 256)
     for s in range(SEQ):
-        stream_st[s] = nt(once, new[s * ROWS : (s + 1) * ROWS]).astype(BF16)
-    skip_st[...] = skip_acc[...].astype(BF16).reshape(SEQ, ROWS, SKIP)
-    store(0, skip_st, skip_out)
-    store(1, stream_st, stream_out)
+        stream_st[s] = nt(once, new[s]).astype(BF16)
+    skip_st[...] = skip_acc[...].astype(BF16)
     weight_sums(4)
     turn((0, 4))
 
     heads[4].wait()
     move(4, 0, ROWS)
-    cotangent(3, 0, ROWS)
-    back(3, 0, ROWS)
+    cotangent(3, 0, DIL[3])
+    back(3, 0, DIL[3])
     heads[3].start()
+    cotangent(3, DIL[3], ROWS)
+    back(3, DIL[3], ROWS)
     for j in (3, 2, 1):
         d = DIL[j]
         move(j, 0, d)
@@ -380,7 +374,6 @@
     move(0, 0, ROWS)
     for s in range(SEQ):
         cot_st[s] = nt(once, flow[s].astype(BF16)).astype(BF16)
-    store(2, cot_st, signal_cot)
     for k in range(2, len(stages)):
         turn((k, 0), (k, 1))
         if k + 1 < len(stages):
@@ -398,22 +391,13 @@
             red_wait(red_send.at[3, j], line_in.at[j, pl.ds(0, ny - 1)])
         red_wait(red_send.at[5, j], final.at[j, pl.ds(0, NX - 1)])
         red_wait(red_send.at[6, j], final.at[j, pl.ds(0, NX)])
-    staged = (skip_st, stream_st, cot_st, past_st, now_st, res_st, gskip_st)
-    outs = (skip_out, stream_out, signal_cot, g_past, g_now, g_res, g_skip)
-    for which in range(7):
-        pltpu.make_async_copy(staged[which], outs[which], out_sem.at[which]).wait()
 
 
 def relay(*refs):
-    ins, outs, held, in_sem, out_sem = refs[:7], refs[7:14], refs[14:21], refs[21], refs[22]
-    loads = [pltpu.make_async_copy(ins[i], held[i], in_sem.at[i]) for i in range(7)]
-    stores = [pltpu.make_async_copy(held[i], outs[i], out_sem.at[i]) for i in range(7)]
-    for copy in loads:
+    copies = [pltpu.make_async_copy(refs[i], refs[7 + i], refs[14].at[i]) for i in range(7)]
+    for copy in copies:
         copy.start()
-    for i in range(7):
-        loads[i].wait()
-        stores[i].start()
-    for copy in stores:
+    for copy in copies:
         copy.wait()
 
 
@@ -424,33 +408,31 @@
         (SEQ, ROWS, SKIP), (SEQ, RES, ROWS), (SEQ, RES, ROWS),
         (LAYERS, RES, 2 * GATE), (LAYERS, RES, 2 * GATE), (LAYERS, RES, GATE), (LAYERS, GATE, SKIP),
     )
-    anywhere = pl.BlockSpec(memory_space=pl.ANY)
-    results = tuple(jax.ShapeDtypeStruct(s, BF16) for s in shapes)
+    hbm = pl.BlockSpec(memory_space=pltpu.HBM)
+    vmem = pl.BlockSpec(memory_space=pltpu.VMEM)
     bf = functools.partial(pltpu.VMEM, dtype=BF16)
     fp = functools.partial(pltpu.VMEM, dtype=F32)
     outs = pl.pallas_call(
         functools.partial(kernel, ny, nz, scale),
-        out_shape=results,
-        in_specs=[anywhere] * 7,
-        out_specs=(anywhere,) * 7,
+        out_shape=tuple(pltpu.VMEM(s, BF16) for s in shapes),
+        in_specs=[hbm] * 7,
+        out_specs=(vmem,) * 7,
         scratch_shapes=[
             bf((SEQ, RES, ROWS)),
             bf((SEQ, RES, ROWS)),
             bf((LAYERS, RES, GATE)),
             bf((SEQ, ROWS, SKIP)),
-            *[bf(s) for s in shapes],
             bf((LAYERS, 128, 512)),
             bf((LAYERS, 256, 512)),
             bf((LAYERS, 256, 256)),
             bf((LAYERS, 256, 256)),
             fp((LAYERS, SEQ, 256, 128)),
-            bf((LAYERS, N, 128)),
+            bf((LAYERS, SEQ, ROWS, 128)),
             fp((N, 512)),
-            bf((N, 256)),
-            bf((LAYERS, N, 256)),
-            fp((LAYERS, N, 256)),
-            fp((LAYERS, N, 256)),
-            fp((N, 128)),
+            bf((LAYERS, SEQ, 256, 256)),
+            fp((LAYERS, SEQ, 256, 256)),
+            fp((LAYERS, SEQ, 256, 256)),
+            fp((SEQ, ROWS, 128)),
             fp((SEQ, ROWS, 128)),
             fp((N, 256)),
             bf((LAYERS, SEQ, ROWS, 128)),
@@ -472,24 +454,29 @@
             pltpu.SemaphoreType.DMA((12,)),
             pltpu.SemaphoreType.DMA((7,)),
             pltpu.SemaphoreType.DMA((7,)),
-            pltpu.SemaphoreType.DMA((7,)),
             pltpu.SemaphoreType.DMA((7, LAYERS)),
             pltpu.SemaphoreType.DMA((7, LAYERS)),
         ],
         compiler_params=pltpu.CompilerParams(
-            collective_id=0, has_side_effects=True, vmem_limit_bytes=60 * 1024 * 1024
+            collective_id=0, has_side_effects=True, vmem_limit_bytes=44 * 1024 * 1024
         ),
     )(
-        jnp.swapaxes(signal, 1, 2), skip_grad, jnp.swapaxes(stream_grad, 1, 2),
-        w_past, w_now, jnp.swapaxes(w_res, 1, 2), w_skip,
+        *(
+            pltpu.with_memory_space_constraint(array, pltpu.HBM)
+            for array in (
+                jnp.swapaxes(signal, 1, 2), skip_grad, jnp.swapaxes(stream_grad, 1, 2),
+                w_past, w_now, jnp.swapaxes(w_res, 1, 2), w_skip,
+            )
+        )
     )
     outs = pl.pallas_call(
         relay,
-        out_shape=results,
-        in_specs=[anywhere] * 7,
-        out_specs=(anywhere,) * 7,
-        scratch_shapes=[*[bf(s) for s in shapes]] + [pltpu.SemaphoreType.DMA((7,))] * 2,
-    )(*outs)
+        out_shape=tuple(pltpu.HBM(s, BF16) for s in shapes),
+        in_specs=[vmem] * 7,
+        out_specs=(hbm,) * 7,
+        scratch_shapes=[pltpu.SemaphoreType.DMA((7,))],
+        compiler_params=pltpu.CompilerParams(vmem_limit_bytes=16 * 1024 * 1024),
+    )(*(pltpu.with_memory_space_constraint(array, pltpu.VMEM) for array in outs))
     skip, stream, cot, g_past, g_now, g_res, g_skip = outs
     return (
         skip, jnp.swapaxes(stream, 1, 2), jnp.swapaxes(cot, 1, 2),

time: 75.9 us -> 71.4 us (0.941)
  Pallas kernels: 75.1 us -> 70.6 us
    pallas_call x2, Pallas kernels: 75.1 us -> 70.6 us  [the longest x1 69.5 us: on_device(): pl.pallas_call(functools.partial(kernel, ny, nz, scale), out_shape=tuple(...]
where the time goes in v3:
time: 71.4 us; the launch traced here: 71.3 us
  Pallas kernels  70.6 us (99%)
    pallas_call x1, Pallas kernels, on_device(): pl.pallas_call(functools.partial(kernel, ny, nz, scale), out_shape=tuple(...  69.5 us

profile of v3, /device:TPU:1, one launch (start us, length us, event | category | flops | bytes accessed | tf_op | source)
XLA Modules:
  0.0 71.3 jit_solution(11503488422512180058)
XLA Ops:
  0.6 69.5 %shard_map.126 = (bf16[4,128,128]{2,1,0:T(8,128)(2,1)S(1)}, bf16[4,64,128]{2,1,0:T(8,128)(2,1)S(1)}, bf16[4,64,128]{2,1,0:T(8,128)(2,1)S(1)}, bf16[5,64,512]{2,1...) custom-call(bf16[4,64,128]{2,1,0:T(8,128)(2,1)} %bitcast.7, ...), custom_call_target="tpu_custom_call" | custom-call | tf_op jit(solution)/shard_map/pallas_call | solution.py:415
  70.1 1.1 %shard_map.127 = (bf16[4,128,128]{2,1,0:T(8,128)(2,1)}, bf16[4,64,128]{2,1,0:T(8,128)(2,1)}, bf16[4,64,128]{2,1,0:T(8,128)(2,1)}, bf16[5,64,512]{2,1,0:T(8,128)(...) custom-call(bf16[4,128,128]{2,1,0:T(8,128)(2,1)S(1)} %get-tuple-element.21.refs_0_, ...), custom_call_target="tpu_custom_call" | custom-call | tf_op jit(solution)/shard_map/pallas_call | solution.py:472

commit v4 on v3

--- a/solution.py
+++ b/solution.py
@@ -141,6 +141,9 @@
     for s in range(SEQ):
         flow[s] = tn(sgrad[s], twice)
 
+    def pack(rows):
+        return jnp.where(low_half, rows[0:2], rows[2:4]).astype(BF16)
+
     def gates(j, lo, hi):
         span = hi - lo
         count = SEQ * span
@@ -187,7 +190,7 @@
         advance(j, LOW[j], LOW[j] + 128)
     gates(3, 128, 256)
     new = advance(3, 128, 256)
-    h4_out[...] = new
+    h4_out[...] = pack(new.astype(F32))
     second = halo_copy(6, h4_out, h4_in, after)
     second.start()
 
@@ -217,8 +220,11 @@
         lax.fori_loop(0, SEQ * per, step, 0)
         both = nt(pcot[j, :, a:b, :].reshape(count, 2 * GATE), wb[j])
         past = both[:, 0:128].astype(BF16).reshape(SEQ, span, 128)
-        past_out[j, :, a:b, :] = past
-        past_f[j, :, a:b, :] = past.astype(F32)
+        past = past.astype(F32)
+        past_f[j, :, a:b, :] = past
+        head = min(b, max(DIL[j], 16))
+        if a < head:
+            past_out[j, :, a:head, :] = pack(past[:, 0 : head - a, :])
         flow[:, a:b, :] += both[:, 128:256].reshape(SEQ, span, 128)
 
     def head_copy(j):
@@ -233,6 +239,10 @@
             pieces.append(past_f[j, :, lo : min(hi, ROWS), :])
         if hi > ROWS:
             edge = past_in[j, :, 0 : max(d, 16), :].astype(F32)
+            turned = pltpu.roll(edge, RES, 2)
+            edge = jnp.concatenate(
+                [jnp.where(low_half, edge, turned), jnp.where(low_half, turned, edge)], 0
+            )
             pieces.append(has_after * edge[:, max(lo - ROWS, 0) : hi - ROWS, :])
         flow[:, a:b, :] += pieces[0] if len(pieces) == 1 else jnp.concatenate(pieces, 1)
 
@@ -278,6 +288,7 @@
             part[j, k // tz, k % tz] = jnp.zeros((16, 128), BF16)
         for r, (z, peer) in enumerate(z_peers):
             red_copy(2, j, part.at[j, z], part_in.at[j, r], peer)
+        red_wait(red_send.at[0, j], pair_in.at[j])
 
     def across_y(j):
         if nz > 1:
@@ -288,6 +299,7 @@
         line_in[j, yi] = total.astype(BF16)
         for _, peer in y_peers:
             red_copy(3, j, line_in.at[j, yi], line_in.at[j, yi], peer)
+        red_wait(red_send.at[1, j], ring_in.at[j])
 
     def gather_z(j):
         if ny > 1:
@@ -298,16 +310,23 @@
         final[j, ei, zi] = (total * scale).astype(BF16)
         for _, peer in z_peers:
             red_copy(4, j, final.at[j, ei, zi], final.at[j, ei, zi], peer)
+        if nz > 1:
+            red_wait(red_send.at[2, j], part_in.at[j])
 
     def gather_x(j):
         if nz > 1:
             red_wait(red_recv.at[4, j], final.at[j, 0, pl.ds(0, nz - 1)])
         for _, peer in x_peers:
             red_copy(5, j, final.at[j, ei], final.at[j, ei], peer)
+        if ny > 1:
+            red_wait(red_send.at[3, j], line_in.at[j, pl.ds(0, ny - 1)])
 
     def gather_core(j):
         red_wait(red_recv.at[5, j], final.at[j, pl.ds(0, NX - 1)])
         red_copy(6, j, final.at[j, mine], final.at[j, mine], sibling)
+        if nz > 1:
+            red_wait(red_send.at[4, j], final.at[j, 0, pl.ds(0, nz - 1)])
+        red_wait(red_send.at[5, j], final.at[j, pl.ds(0, NX - 1)])
 
     def finish(j):
         red_wait(red_recv.at[6, j], final.at[j, pl.ds(0, NX)])
@@ -319,6 +338,7 @@
         res_st[j, :, 128:256] = tile[4][64:128]
         gskip_st[j, 0:128, :] = tile[5]
         gskip_st[j, 128:256, :] = tile[6]
+        red_wait(red_send.at[6, j], final.at[j, pl.ds(0, NX)])
 
     stages = (
         scatter_core, scatter_x, scatter_z, across_y, gather_z, gather_x, gather_core, finish
@@ -330,7 +350,9 @@
 
     cotangent(4, 0, ROWS)
     second.wait()
-    h2[4, :, 0:128, :] = has_before * h4_in[...].astype(F32)
+    arrived = has_before * h4_in[...].astype(F32)
+    h2[4, 0:2, 0:128, :] = arrived
+    h2[4, 2:4, 0:128, :] = pltpu.roll(arrived, RES, 2)
     gates(4, 128, 256)
     heads = [head_copy(j) for j in range(LAYERS)]
     back(4, 0, ROWS)
@@ -381,17 +403,6 @@
         if k + 2 < len(stages):
             turn((k + 2, 4))
 
-    for j in range(LAYERS):
-        red_wait(red_send.at[0, j], pair_in.at[j])
-        red_wait(red_send.at[1, j], ring_in.at[j])
-        if nz > 1:
-            red_wait(red_send.at[2, j], part_in.at[j])
-            red_wait(red_send.at[4, j], final.at[j, 0, pl.ds(0, nz - 1)])
-        if ny > 1:
-            red_wait(red_send.at[3, j], line_in.at[j, pl.ds(0, ny - 1)])
-        red_wait(red_send.at[5, j], final.at[j, pl.ds(0, NX - 1)])
-        red_wait(red_send.at[6, j], final.at[j, pl.ds(0, NX)])
-
 
 def relay(*refs):
     copies = [pltpu.make_async_copy(refs[i], refs[7 + i], refs[14].at[i]) for i in range(7)]
@@ -438,11 +449,11 @@
             bf((LAYERS, SEQ, ROWS, 128)),
             bf((LAYERS, SEQ, ROWS, 512)),
             bf((SEQ, RES, ROWS)),
-            bf((SEQ, ROWS, 128)),
-            bf((SEQ, ROWS, 128)),
+            bf((2, ROWS, 128)),
+            bf((2, ROWS, 128)),
             fp((LAYERS, SEQ, ROWS, 128)),
-            bf((LAYERS, SEQ, ROWS, 128)),
-            bf((LAYERS, SEQ, ROWS, 128)),
+            bf((LAYERS, 2, ROWS, 128)),
+            bf((LAYERS, 2, ROWS, 128)),
             bf((LAYERS, 2 * NX, 16, 896)),
             bf((LAYERS, NX, 16, 896)),
             bf((LAYERS, NX, 16, 896)),

time: 71.4 us -> 68.3 us (0.957)
  Pallas kernels: 70.6 us -> 67.5 us
    pallas_call x1, Pallas kernels: 69.5 us -> 66.3 us  [on_device(): pl.pallas_call(functools.partial(kernel, ny, nz, scale), out_shape=tuple(...]
where the time goes in v4:
time: 68.3 us; the launch traced here: 68.1 us
  Pallas kernels  67.5 us (99%)
    pallas_call x1, Pallas kernels, on_device(): pl.pallas_call(functools.partial(kernel, ny, nz, scale), out_shape=tuple(...  66.3 us

profile of v4, /device:TPU:1, one launch (start us, length us, event | category | flops | bytes accessed | tf_op | source)
XLA Modules:
  0.0 68.1 jit_solution(15226393310549997143)
XLA Ops:
  0.6 66.3 %shard_map.126 = (bf16[4,128,128]{2,1,0:T(8,128)(2,1)S(1)}, bf16[4,64,128]{2,1,0:T(8,128)(2,1)S(1)}, bf16[4,64,128]{2,1,0:T(8,128)(2,1)S(1)}, bf16[5,64,512]{2,1...) custom-call(bf16[4,64,128]{2,1,0:T(8,128)(2,1)} %bitcast.7, ...), custom_call_target="tpu_custom_call" | custom-call | tf_op jit(solution)/shard_map/pallas_call | solution.py:426
  67.0 1.1 %shard_map.127 = (bf16[4,128,128]{2,1,0:T(8,128)(2,1)}, bf16[4,64,128]{2,1,0:T(8,128)(2,1)}, bf16[4,64,128]{2,1,0:T(8,128)(2,1)}, bf16[5,64,512]{2,1,0:T(8,128)(...) custom-call(bf16[4,128,128]{2,1,0:T(8,128)(2,1)S(1)} %get-tuple-element.21.refs_0_, ...), custom_call_target="tpu_custom_call" | custom-call | tf_op jit(solution)/shard_map/pallas_call | solution.py:483

commit v5 on v4

--- a/solution.py
+++ b/solution.py
@@ -63,6 +63,7 @@
     yi = tm // (2 * nz)
     ei = core * NX + xi
     tz = TILES // nz
+    filled = pl.ds(0, -(-WIRE // tz))
 
     after = {"tm": (tm + 1) % blocks, "batch": batch}
     before = {"tm": (tm + blocks - 1) % blocks, "batch": batch}
@@ -317,19 +318,19 @@
         if nz > 1:
             red_wait(red_recv.at[4, j], final.at[j, 0, pl.ds(0, nz - 1)])
         for _, peer in x_peers:
-            red_copy(5, j, final.at[j, ei], final.at[j, ei], peer)
+            red_copy(5, j, final.at[j, ei, filled], final.at[j, ei, filled], peer)
         if ny > 1:
             red_wait(red_send.at[3, j], line_in.at[j, pl.ds(0, ny - 1)])
 
     def gather_core(j):
-        red_wait(red_recv.at[5, j], final.at[j, pl.ds(0, NX - 1)])
-        red_copy(6, j, final.at[j, mine], final.at[j, mine], sibling)
+        red_wait(red_recv.at[5, j], final.at[j, pl.ds(0, NX - 1), filled])
+        red_copy(6, j, final.at[j, mine, filled], final.at[j, mine, filled], sibling)
         if nz > 1:
             red_wait(red_send.at[4, j], final.at[j, 0, pl.ds(0, nz - 1)])
-        red_wait(red_send.at[5, j], final.at[j, pl.ds(0, NX - 1)])
+        red_wait(red_send.at[5, j], final.at[j, pl.ds(0, NX - 1), filled])
 
     def finish(j):
-        red_wait(red_recv.at[6, j], final.at[j, pl.ds(0, NX)])
+        red_wait(red_recv.at[6, j], final.at[j, pl.ds(0, NX), filled])
         tile = [final[j, :, k // tz, k % tz].reshape(128, 128) for k in range(WIRE)]
         for k in range(4):
             past_st[j, :, 128 * k : 128 * k + 128] = tile[k][0:64]
@@ -338,7 +339,7 @@
         res_st[j, :, 128:256] = tile[4][64:128]
         gskip_st[j, 0:128, :] = tile[5]
         gskip_st[j, 128:256, :] = tile[6]
-        red_wait(red_send.at[6, j], final.at[j, pl.ds(0, NX)])
+        red_wait(red_send.at[6, j], final.at[j, pl.ds(0, NX), filled])
 
     stages = (
         scatter_core, scatter_x, scatter_z, across_y, gather_z, gather_x, gather_core, finish

time: 68.3 us -> 68.1 us (level)
  no operation moved by 1% of the time
where the time goes in v5:
time: 68.1 us; the launch traced here: 67.9 us
  Pallas kernels  67.3 us (99%)
    pallas_call x1, Pallas kernels, on_device(): pl.pallas_call(functools.partial(kernel, ny, nz, scale), out_shape=tuple(...  66.1 us

profile of v5, /device:TPU:1, one launch (start us, length us, event | category | flops | bytes accessed | tf_op | source)
XLA Modules:
  0.0 67.9 jit_solution(15383818002292663376)
XLA Ops:
  0.6 66.1 %shard_map.126 = (bf16[4,128,128]{2,1,0:T(8,128)(2,1)S(1)}, bf16[4,64,128]{2,1,0:T(8,128)(2,1)S(1)}, bf16[4,64,128]{2,1,0:T(8,128)(2,1)S(1)}, bf16[5,64,512]{2,1...) custom-call(bf16[4,64,128]{2,1,0:T(8,128)(2,1)} %bitcast.7, ...), custom_call_target="tpu_custom_call" | custom-call | tf_op jit(solution)/shard_map/pallas_call | solution.py:427
  66.8 1.1 %shard_map.127 = (bf16[4,128,128]{2,1,0:T(8,128)(2,1)}, bf16[4,64,128]{2,1,0:T(8,128)(2,1)}, bf16[4,64,128]{2,1,0:T(8,128)(2,1)}, bf16[5,64,512]{2,1,0:T(8,128)(...) custom-call(bf16[4,128,128]{2,1,0:T(8,128)(2,1)S(1)} %get-tuple-element.21.refs_0_, ...), custom_call_target="tpu_custom_call" | custom-call | tf_op jit(solution)/shard_map/pallas_call | solution.py:484
